TPU v7x, 256 devices: a whole 4x4x8 slice. The times are simulated.
256 devices in a mesh: ctx: 64 (over x, z, y_hi), uly: 4 (over y_lo, core).
Axes of the slice: x: 4, y: 4 (y_hi: 2, y_lo: 2; y = y_hi * 2 + y_lo), z: 8, core: 2. Of those that a mesh axis runs over, the one named last changes fastest.
Arguments:
- query_rows: bfloat16 [32768, 2560], P(('ctx', 'uly')), may hold values from -8 to 8
- key_rows: bfloat16 [32768, 2560], P(('ctx', 'uly')), may hold values from -8 to 8
- value_rows: bfloat16 [32768, 2560], P(('ctx', 'uly')), may hold values from -6 to 6
- query_tan: bfloat16 [32768, 2560], P(('ctx', 'uly')), may hold values from -6 to 6
- key_tan: bfloat16 [32768, 2560], P(('ctx', 'uly')), may hold values from -6 to 6
- value_tan: bfloat16 [32768, 2560], P(('ctx', 'uly')), may hold values from -6 to 6
- tile_query: int32 [64, 64], P('ctx'), may hold values from 0 to 3, as said below
- tile_key: int32 [64, 64], P('ctx'), may hold values from 0 to 15, as said below
- tile_count: int32 [64], P('ctx'), may hold values from 8 to 64
Outputs:
- attended: bfloat16 [32768, 2560], P(('ctx', 'uly'))
- attended_tan: bfloat16 [32768, 2560], P(('ctx', 'uly'))
Inputs may be any that keep to these rules, and one draw needn't show every extreme that they name: `tile_query`: only the first tile_count[b] entries of row b are listed; pairs in a row are distinct. `tile_key`: A key code c names tile c % 4 of the block c // 4 places before the query's block, going round the loop of 64 blocks.
All inputs are finite; a program needn't handle non-finite values.
Results may differ from a plain program's by a relative error of at most 0.012.
The roundings to bfloat16 on the way count: a program that leaves them out, or rounds other values in their place, can miss the bound.
Values may be sent and summed in bfloat16 or wider, within the bound.
A program may use at most 128 MiB of HBM per device.

v0:
```python
import jax
import jax.numpy as jnp
from jax import lax
from jax.sharding import PartitionSpec as P

HEAD = 128
TILE = 128
REACH = 4
MAXT = 64


def shifted(block, axis, distance):
    devices = range(lax.axis_size(axis))
    route = [((i - distance) % len(devices), i) for i in devices]
    return lax.ppermute(block, axis, route)


def tile_allowed(query_tiles, key_tiles, used_count, tile_rows):
    key_span = REACH * tile_rows
    in_use = jnp.arange(MAXT) < used_count
    pair_code = query_tiles * key_span + key_tiles
    listed = jnp.any(
        (pair_code[:, None] == jnp.arange(tile_rows * key_span)[None, :]) & in_use[:, None], axis=0
    )
    listed = listed.reshape(tile_rows, key_span)
    own_tile = jnp.arange(key_span)[None, :] == jnp.arange(tile_rows)[:, None]
    return listed | own_tile


def on_device(
    query_rows,
    key_rows,
    value_rows,
    query_tan,
    key_tan,
    value_tan,
    tile_query,
    tile_key,
    tile_count,
):
    stacked = jnp.stack([query_rows, query_tan, key_rows, value_rows, key_tan, value_tan])
    grouped = lax.all_to_all(stacked, "uly", split_axis=2, concat_axis=1, tiled=True)
    block_rows = grouped.shape[1]
    feature_cols = grouped.shape[2]
    local_heads = feature_cols // HEAD
    tiles_here = block_rows // TILE
    allowed = tile_allowed(tile_query[0], tile_key[0], tile_count[0], tiles_here)
    queries = grouped[0].reshape(block_rows, local_heads, HEAD)
    tan_queries = grouped[1].reshape(block_rows, local_heads, HEAD)
    own_band = grouped[2:]
    scaling = HEAD ** (-0.5)
    start_state = (
        jnp.full((local_heads, block_rows), -1e30, jnp.float32),
        jnp.zeros((local_heads, block_rows), jnp.float32),
        jnp.zeros((local_heads, block_rows), jnp.float32),
        jnp.zeros((local_heads, block_rows, HEAD), jnp.float32),
        jnp.zeros((local_heads, block_rows, HEAD), jnp.float32),
    )

    def absorb(carried, band_block, behind):
        run_max, weight_sum, linear, primal, tangent = carried
        tile_band = allowed[:, behind * tiles_here : (behind + 1) * tiles_here]
        token_mask = jnp.repeat(jnp.repeat(tile_band, TILE, 0), TILE, 1)[None]
        keys_here = band_block[0].reshape(block_rows, local_heads, HEAD)
        values_here = band_block[1].reshape(block_rows, local_heads, HEAD)
        tan_keys = band_block[2].reshape(block_rows, local_heads, HEAD)
        tan_values = band_block[3].reshape(block_rows, local_heads, HEAD)
        scores = scaling * jnp.einsum(
            "qhd,khd->hqk", queries, keys_here, preferred_element_type=jnp.float32
        )
        score_tan = scaling * (
            jnp.einsum("qhd,khd->hqk", tan_queries, keys_here, preferred_element_type=jnp.float32)
            + jnp.einsum("qhd,khd->hqk", queries, tan_keys, preferred_element_type=jnp.float32)
        )
        new_max = jnp.maximum(run_max, jnp.max(jnp.where(token_mask, scores, -1e30), axis=2))
        rescale = jnp.exp(run_max - new_max)
        weights = jnp.where(token_mask, jnp.exp(scores - new_max[..., None]), 0.0)
        product = weights * score_tan
        weights_low = weights.astype(jnp.bfloat16)
        product_low = product.astype(jnp.bfloat16)
        weight_sum = weight_sum * rescale + jnp.sum(weights, axis=2)
        linear = linear * rescale + jnp.sum(product, axis=2)
        primal = primal * rescale[..., None] + jnp.einsum(
            "hqk,khd->hqd", weights_low, values_here, preferred_element_type=jnp.float32
        )
        tangent = (
            tangent * rescale[..., None]
            + jnp.einsum(
                "hqk,khd->hqd", product_low, values_here, preferred_element_type=jnp.float32
            )
            + jnp.einsum(
                "hqk,khd->hqd", weights_low, tan_values, preferred_element_type=jnp.float32
            )
        )
        return (new_max, weight_sum, linear, primal, tangent)

    def visit_block(carried, band_block, behind):
        return absorb(carried, band_block, behind)

    carried = visit_block(start_state, own_band, 0)
    passing = own_band
    for behind in range(1, REACH):
        passing = shifted(passing, "ctx", 1)
        carried = visit_block(carried, passing, behind)
    run_max, weight_sum, linear, primal, tangent = carried
    primal = primal / weight_sum[..., None]
    tangent = (tangent - linear[..., None] * primal) / weight_sum[..., None]
    merged = jnp.stack([primal, tangent]).astype(jnp.bfloat16)
    merged = jnp.transpose(merged, (0, 2, 1, 3)).reshape(2, block_rows, feature_cols)
    returned = lax.all_to_all(merged, "uly", split_axis=1, concat_axis=2, tiled=True)
    return (returned[0], returned[1])


def solution(mesh):
    return jax.shard_map(
        on_device,
        mesh=mesh,
        in_specs=(
            P(("ctx", "uly"), None),
            P(("ctx", "uly"), None),
            P(("ctx", "uly"), None),
            P(("ctx", "uly"), None),
            P(("ctx", "uly"), None),
            P(("ctx", "uly"), None),
            P("ctx", None),
            P("ctx", None),
            P("ctx"),
        ),
        out_specs=(P(("ctx", "uly"), None), P(("ctx", "uly"), None)),
        check_vma=False,
    )
```

profile of v0, /device:TPU:1, one launch (start us, length us, event | category | flops | bytes accessed | tf_op | source)
XLA Modules:
  0.0 364.8 jit_solution(7998261782524454753)
XLA Ops:
  0.6 2.1 bitcast_dynamic-update-slice_fusion.5
  2.7 2.0 bitcast_dynamic-update-slice_fusion.4
  4.7 2.0 bitcast_dynamic-update-slice_fusion.3
  6.7 2.0 bitcast_dynamic-update-slice_fusion.2
  10.6 7.7 %copy.167 = bf16[6,128,2560]{1,0,2:T(8,128)(2,1)} copy(bf16[6,128,2560]{2,1,0:T(8,128)(2,1)} %bitcast_dynamic-update-slice_fusion) | data formatting | bytes 7864320 | tf_op jit(solution)/shard_map/stack | solution.py:41
  18.3 65.5 %all_to_all.30 = bf16[6,128,2560]{1,0,2:T(8,128)(2,1)S(1)} all-to-all(bf16[6,128,2560]{1,0,2:T(8,128)(2,1)} %copy.167), channel_id=1, replica_groups=mesh['ctx'=64,'uly'=4] {'uly'}, dimensions={2} | all-to-all | bytes 7864320 | tf_op jit(solution)/shard_map/all_to_all | solution.py:42
  83.7 3.0 copy.258
  86.8 1.9 copy-done
  89.5 3.1 slice.96
  93.8 64.0 %collective-permute-done = bf16[4,512,640]{1,2,0:T(8,128)(2,1)} collective-permute-done((bf16[4,512,640]{1,2,0:T(8,128)(2,1)}, bf16[4,512,640]{1,2,0:T(8,128)(2,1)}, u32[]{:S(2)}, u32[]{:S(2)}) %collective-permute-start) | collective-permute-done | bytes 2621472 | tf_op jit(solution)/shard_map/ppermute | solution.py:15
  159.5 3.7 %fusion.83 = (bf16[1,4,128,640]{2,1,3,0:T(4,128)(2,1)S(1)}, bf16[1,4,128,640]{2,1,3,0:T(4,128)(2,1)S(1)}, bf16[1,4,128,640]{2,1,3,0:T(4,128)(2,1)S(1)}, bf16[1,4...) fusion(bf16[6,4,128,640]{2,1,3,0:T(4,128)(2,1)} %bitcast.135), kind=kLoop, calls=%fused_computation.88 | loop fusion | bytes 7864320 | tf_op jit(solution)/shard_map/slice | solution.py:67
  165.1 55.5 %collective-permute-done.1 = bf16[4,512,640]{1,2,0:T(8,128)(2,1)} collective-permute-done((bf16[4,512,640]{1,2,0:T(8,128)(2,1)}, bf16[4,512,640]{1,2,0:T(8,128)(2,1)}, u32[]{:S(2)}, u32[]{:S(2)}) %collective-permute-start.1) | collective-permute-done | bytes 2621472 | tf_op jit(solution)/shard_map/ppermute | solution.py:15
  220.7 3.2 fusion.93
  230.0 2.8 fusion.84
  234.8 3.0 fusion.85
  237.9 3.3 fusion.95
  242.4 40.1 %collective-permute-done.2 = bf16[4,512,640]{1,2,0:T(8,128)(2,1)} collective-permute-done((bf16[4,512,640]{1,2,0:T(8,128)(2,1)}, bf16[4,512,640]{1,2,0:T(8,128)(2,1)}, u32[]{:S(2)}, u32[]{:S(2)}) %collective-permute-start.2) | collective-permute-done | bytes 2621472 | tf_op jit(solution)/shard_map/ppermute | solution.py:15
  282.5 3.0 fusion.86
  285.5 3.2 fusion.96
  290.0 5.8 %fusion.89 = (f32[5,512]{1,0:T(8,128)}, bf16[5,512,512]{1,2,0:T(8,128)(2,1)}) fusion(f32[5,512,512]{1,2,0:T(8,128)} %fusion.96, bf16[512,5,128]{0,2,1:T(8,128)(2,1)S(1)} %reshape_squeeze.63, bf16[512,5,128]{0,2,1:T(8,128)(2,1)S(1)} %bitcast.145, f32[5,512]{1,0:T(8,128)S(1)} %get-tuple-element.6, f32[5,512,512]{1,2,0:T(8,128)S(1)} %get-tuple-element.37, ...), kind=kOutput, calls=%fused_computation.94 | convolution fusion | flops 346027520 | bytes 14700544 | tf_op jit(solution)/shard_map/qhd,khd->hqk/dot_general | solution.py:72
  295.8 2.8 fusion.4
  298.7 6.0 %fusion.90 = (f32[5,512]{1,0:T(8,128)}, bf16[5,512,512]{1,2,0:T(8,128)(2,1)}) fusion(f32[5,512,512]{1,2,0:T(8,128)} %fusion.95, bf16[512,5,128]{0,2,1:T(8,128)(2,1)S(1)} %reshape_squeeze.63, bf16[512,5,128]{0,2,1:T(8,128)(2,1)S(1)} %bitcast.143, f32[5,512]{1,0:T(8,128)S(1)} %get-tuple-element.7, f32[5,512,512]{1,2,0:T(8,128)S(1)} %get-tuple-element.39, ...), kind=kOutput, calls=%fused_computation.95 | convolution fusion | flops 346027520 | bytes 14700544 | tf_op jit(solution)/shard_map/qhd,khd->hqk/dot_general | solution.py:72
  304.7 2.4 fusion.70
  307.1 2.3 fusion.73
  309.5 3.5 fusion.91
  313.0 2.4 fusion.76
  315.4 2.2 fusion
  317.7 2.4 fusion.79
  320.1 2.5 fusion.92
  322.8 2.1 fusion.54
  335.0 1.9 copy.208
  336.9 22.2 %all_to_all.31 = bf16[2,512,640]{2,0,1:T(2,128)(2,1)S(1)} all-to-all(bf16[2,512,640]{2,0,1:T(2,128)(2,1)S(1)} %copy.208), channel_id=1, replica_groups=mesh['ctx'=64,'uly'=4] {'uly'}, dimensions={1} | all-to-all | bytes 2621440 | tf_op jit(solution)/shard_map/all_to_all | solution.py:110
  (132 shorter events, 33.0 us)
Async XLA Ops:
  0.6 8.0 %copy-start.18 = (bf16[128,2560]{1,0:T(8,128)(2,1)S(1)}, bf16[128,2560]{1,0:T(8,128)(2,1)}, u32[]{:S(2)}) copy-start(bf16[128,2560]{1,0:T(8,128)(2,1)} %param.13) | copy-start | bytes 1966084
  0.6 9.0 %copy-start.19 = (bf16[128,2560]{1,0:T(8,128)(2,1)S(1)}, bf16[128,2560]{1,0:T(8,128)(2,1)}, u32[]{:S(2)}) copy-start(bf16[128,2560]{1,0:T(8,128)(2,1)} %param.14) | copy-start | bytes 1966084
  88.6 69.8 %copy-start.33 = (s32[1,64]{1,0:T(1,128)S(1)}, s32[1,64]{1,0:T(1,128)}, u32[]{:S(2)}) copy-start(s32[1,64]{1,0:T(1,128)} %param.16) | copy-start | bytes 772
  88.6 69.8 %copy-start.34 = (s32[1,64]{1,0:T(1,128)S(1)}, s32[1,64]{1,0:T(1,128)}, u32[]{:S(2)}) copy-start(s32[1,64]{1,0:T(1,128)} %param.15) | copy-start | bytes 772
  92.6 65.2 %collective-permute-start = (bf16[4,512,640]{1,2,0:T(8,128)(2,1)}, bf16[4,512,640]{1,2,0:T(8,128)(2,1)}, u32[]{:S(2)}, u32[]{:S(2)}) collective-permute-start(bf16[4,512,640]{1,2,0:T(8,128)(2,1)} %slice.96), channel_id=1, source_target_pairs={{252,0},{0,4},{4,8},{8,12},{12,16},{16,20},{20,24},{24,28},{28,32}... | collective-permute-start | bytes 7864328 | tf_op jit(solution)/shard_map/ppermute | solution.py:15
  157.8 62.8 %collective-permute-start.1 = (bf16[4,512,640]{1,2,0:T(8,128)(2,1)}, bf16[4,512,640]{1,2,0:T(8,128)(2,1)}, u32[]{:S(2)}, u32[]{:S(2)}) collective-permute-start(bf16[4,512,640]{1,2,0:T(8,128)(2,1)} %collective-permute-done), channel_id=1, source_target_pairs={{252,0},{0,4},{4,8},{8,12},{12,16},{16,20},{20,24},{24,28},{28,32}... | collective-permute-start | bytes 7864328 | tf_op jit(solution)/shard_map/ppermute | solution.py:15
  220.5 62.0 %collective-permute-start.2 = (bf16[4,512,640]{1,2,0:T(8,128)(2,1)}, bf16[4,512,640]{1,2,0:T(8,128)(2,1)}, u32[]{:S(2)}, u32[]{:S(2)}) collective-permute-start(bf16[4,512,640]{1,2,0:T(8,128)(2,1)} %collective-permute-done.1), channel_id=1, source_target_pairs={{252,0},{0,4},{4,8},{8,12},{12,16},{16,20},{20,24},{24,28},{28,32}... | collective-permute-start | bytes 7864328 | tf_op jit(solution)/shard_map/ppermute | solution.py:15
  229.9 60.0 %copy-start.26 = (f32[5,512]{1,0:T(8,128)}, f32[5,512]{1,0:T(8,128)S(1)}, u32[]{:S(2)}) copy-start(f32[5,512]{1,0:T(8,128)S(1)} %get-tuple-element.42) | copy-start | bytes 30724
  241.2 65.9 %copy-start.3 = (pred[512,4,128]{0,2,1:T(8,128)(4,1)}, pred[512,4,128]{0,2,1:T(8,128)(4,1)S(1)}, u32[]{:S(2)}) copy-start(pred[512,4,128]{0,2,1:T(8,128)(4,1)S(1)} %broadcast_in_dim.115) | copy-start | bytes 786436
  288.8 15.9 %copy-start.5 = (pred[512,4,128]{0,2,1:T(8,128)(4,1)}, pred[512,4,128]{0,2,1:T(8,128)(4,1)S(1)}, u32[]{:S(2)}) copy-start(pred[512,4,128]{0,2,1:T(8,128)(4,1)S(1)} %broadcast_in_dim.119) | copy-start | bytes 786436
  290.0 17.1 %copy-start.21 = (f32[5,512]{1,0:T(8,128)}, f32[5,512]{1,0:T(8,128)S(1)}, u32[]{:S(2)}) copy-start(f32[5,512]{1,0:T(8,128)S(1)} %get-tuple-element.7) | copy-start | bytes 30724
  290.0 25.4 %copy-start.24 = (f32[5,512]{1,0:T(8,128)}, f32[5,512]{1,0:T(8,128)S(1)}, u32[]{:S(2)}) copy-start(f32[5,512]{1,0:T(8,128)S(1)} %get-tuple-element.8) | copy-start | bytes 30724
  290.0 30.0 %copy-start.28 = (f32[5,512]{1,0:T(8,128)}, f32[5,512]{1,0:T(8,128)S(1)}, u32[]{:S(2)}) copy-start(f32[5,512]{1,0:T(8,128)S(1)} %get-tuple-element.31) | copy-start | bytes 30724
  298.7 6.1 %copy-start.17 = (bf16[1,512,640]{1,2,0:T(8,128)(2,1)S(1)}, bf16[1,512,640]{1,2,0:T(8,128)(2,1)}, u32[]{:S(2)}) copy-start(bf16[1,512,640]{1,2,0:T(8,128)(2,1)} %get-tuple-element.23) | copy-start | bytes 1966084
  304.7 2.4 copy-start.16
  312.9 7.1 %slice-start = ((s8[5242880]{0:T(1024)(128)(4,1)}), s8[4194304]{0:T(1024)(128)(4,1)S(1)}, s32[]{:S(2)}) async-start(s8[5242880]{0:T(1024)(128)(4,1)} %bitcast.136), calls=%async_computation.2 | async-start | bytes 8388608
  315.4 2.3 copy-start.20
  315.4 4.6 %slice-start.1 = ((s8[5242880]{0:T(1024)(128)(4,1)}), s8[1048576]{0:T(1024)(128)(4,1)S(1)}, s32[]{:S(2)}) async-start(s8[5242880]{0:T(1024)(128)(4,1)} %bitcast.136), calls=%async_computation.3 | async-start | bytes 2097152
  317.7 2.4 copy-start.7
  320.1 2.6 copy-start.22
  320.1 2.6 copy-start.25
  320.1 2.6 copy-start.27
  320.1 2.6 copy-start.31
  320.1 2.6 copy-start.32
  320.1 2.6 copy-start.29
  320.1 2.6 copy-start.30
  320.1 2.6 copy-start.11
  322.6 2.3 copy-start.9
  329.3 2.1 copy-start.13
  329.4 2.8 copy-start.1
  329.4 3.1 copy-start.12
  332.0 2.2 copy-start.35
  (9 other events, 14.2 us)
where the time goes:
time: 372 us; the launch traced here: 365 us
  waiting for transfers between devices  160 us (43%)
  blocking collectives  87.6 us (24%)
  local copies, waits for them, and re-layouts  57.1 us (15%)
  matrix products  51.3 us (14%)
  other arithmetic  5.48 us (1%)
    ppermute x3, waiting for transfers between devices, shifted(): return lax.ppermute(block, axis, route)  160 us
    all_to_all x1, blocking collectives, on_device(): lax.all_to_all(stacked, 'uly', split_axis=2, concat_axis=1, tiled=True)  65.5 us
    all_to_all x1, blocking collectives, on_device(): lax.all_to_all(merged, 'uly', split_axis=1, concat_axis=2, tiled=True)  22.2 us
    dot_general x4, matrix products, absorb(): jnp.einsum('qhd,khd->hqk', tan_queries, keys_here, preferred_element_type...  18.6 us
    unnamed x91, local copies, waits for them, and re-layouts  16.1 us
    slice x4, local copies, waits for them, and re-layouts, absorb(): tan_values = band_block[3].reshape(block_rows, local_heads, HEAD)  12.5 us
    dot_general x4, matrix products, absorb(): jnp.einsum('qhd,khd->hqk', queries, tan_keys, preferred_element_type=jnp....  9.85 us
    dot_general x4, matrix products, absorb(): jnp.einsum('hqk,khd->hqd', weights_low, tan_values, preferred_element_typ...  9.54 us
  transfers between devices with their start and end apart: 3, of which 3 were waited for; matrix products, arithmetic and copies ran while one was open for 8% of the time, Pallas kernels for 0%

commit v1 on v0

v1 whole, which is shorter than its diff:
```python
import functools
import math
import jax
import jax.numpy as jnp
from jax import lax
from jax.experimental import pallas as pl
from jax.experimental.pallas import tpu as pltpu
from jax.sharding import PartitionSpec as P

HEAD = 128
TILE = 128
REACH = 4
MAXT = 64
LOCAL_HEADS = 5
CT = 512
QT = 4
ROWS = 256
MESH = pl.DeviceIdType.MESH
SCALING = HEAD ** (-0.5)
LOG2E = math.log2(math.e)
NEG = -1e30


def attend(query, keyval, bias, state_max, state_sum, state_lin, acc_w, acc_p, j, slot):
    per = ROWS // TILE
    for i in range(CT // ROWS):
        rows = pl.ds(i * ROWS, ROWS)
        q2 = query[j, rows, :]
        scores = lax.dot_general(
            query[j, rows, HEAD:], keyval[j, slot, 0, :, :HEAD], (((1,), (1,)), ((), ())), preferred_element_type=jnp.float32
        )
        tans = lax.dot_general(
            q2, keyval[j, slot, 0], (((1,), (1,)), ((), ())), preferred_element_type=jnp.float32
        )
        masked = []
        for t in range(per):
            wide = jnp.concatenate([bias[i * per + t, slot, c] for c in range(QT)], axis=1)
            masked.append(jnp.concatenate([wide] * (TILE // 8), axis=0))
        scores = scores * (SCALING * LOG2E) + jnp.concatenate(masked, axis=0)
        old_max = state_max[rows, :]
        new_max = jnp.maximum(old_max, jnp.max(scores, axis=1, keepdims=True))
        alpha = jnp.exp2(old_max - new_max)
        weights = jnp.exp2(scores - new_max[:, :1])
        product = weights * tans
        state_max[rows, :] = new_max
        state_sum[rows, :] = state_sum[rows, :] * alpha + jnp.sum(weights, axis=1, keepdims=True)
        state_lin[rows, :] = state_lin[rows, :] * alpha + jnp.sum(product, axis=1, keepdims=True)
        low = weights.astype(jnp.bfloat16)
        prod_low = product.astype(jnp.bfloat16)
        acc_w[rows, :] = acc_w[rows, :] * alpha[:, :1] + jnp.dot(
            low, keyval[j, slot, 1], preferred_element_type=jnp.float32
        )
        acc_p[rows, :] = acc_p[rows, :] * alpha + jnp.dot(
            prod_low, keyval[j, slot, 1, :, :HEAD], preferred_element_type=jnp.float32
        )


def kernel(
    n_ctx,
    q_ref,
    k_ref,
    v_ref,
    qt_ref,
    kt_ref,
    vt_ref,
    tq_ref,
    tk_ref,
    cnt_ref,
    out_p,
    out_t,
    query,
    keyval,
    bias_own,
    bias,
    st_max,
    st_sum,
    st_lin,
    acc_w,
    acc_p,
    outbuf,
    in_send,
    q_recv,
    kv_recv,
    z1_send,
    z2_send,
    xa_send,
    xb_send,
    bias_send,
    bias_recv,
    out_send,
    out_recv,
):
    ctx = lax.axis_index("ctx")
    uly = lax.axis_index("uly")
    core = lax.rem(uly, 2)
    yh = lax.rem(ctx, 2)
    base = ctx - yh
    y = yh * 2 + lax.div(uly, 2)
    other = uly + 1 - 2 * core
    ahead = lax.rem(ctx + 2, n_ctx)
    behind = lax.rem(ctx + n_ctx - 2, n_ctx)
    at_home = core == yh

    barrier = pltpu.get_barrier_semaphore()
    for step in range(1, 8):
        place = lax.rem(yh * 4 + uly + step, 8)
        pl.semaphore_signal(
            barrier, inc=1, device_id=(base + lax.div(place, 4), lax.rem(place, 4)), device_id_type=MESH
        )
    for where in (ahead, behind):
        for who in (uly, other):
            pl.semaphore_signal(barrier, inc=1, device_id=(where, who), device_id_type=MESH)

    lane = lax.broadcasted_iota(jnp.int32, (8, MAXT), 1)
    codes = jnp.broadcast_to(tk_ref[...], (8, MAXT))
    usable = (lane < cnt_ref[0]) & (jnp.broadcast_to(tq_ref[...], (8, MAXT)) == uly)
    for n in range(REACH):
        for c in range(QT):
            seen = jnp.max(jnp.where(usable & (codes == n * QT + c), 1.0, 0.0), axis=1, keepdims=True)
            if n == 0:
                seen = jnp.maximum(seen, jnp.where(uly == c, 1.0, 0.0))
            bias_own[n, c] = jnp.broadcast_to((1.0 - seen) * NEG, (8, HEAD))

    pl.semaphore_wait(barrier, 11)

    own_rows = pl.ds(pl.multiple_of(uly * TILE, TILE), TILE)
    low_half, high_half = pl.ds(0, HEAD), pl.ds(HEAD, HEAD)

    def group_device(place):
        return (base + lax.div(place, 2), lax.rem(place, 2) * 2 + yh)

    def send_in(j):
        for step in range(4):
            place = lax.rem(y + step, 4)
            cols = pl.ds(pl.multiple_of((place * LOCAL_HEADS + j) * HEAD, HEAD), HEAD)
            moves = (
                (k_ref, keyval.at[j, 0, 0, own_rows, low_half], kv_recv.at[j, 0]),
                (kt_ref, keyval.at[j, 0, 0, own_rows, high_half], kv_recv.at[j, 0]),
                (v_ref, keyval.at[j, 0, 1, own_rows, low_half], kv_recv.at[j, 0]),
                (vt_ref, keyval.at[j, 0, 1, own_rows, high_half], kv_recv.at[j, 0]),
                (q_ref, query.at[j, own_rows, high_half], q_recv.at[j]),
                (qt_ref, query.at[j, own_rows, low_half], q_recv.at[j]),
            )

            def remote():
                for a, (src, dst, sem) in enumerate(moves):
                    pltpu.make_async_remote_copy(
                        src_ref=src.at[:, cols],
                        dst_ref=dst,
                        send_sem=in_send.at[step, a],
                        recv_sem=sem,
                        device_id=group_device(place),
                        device_id_type=MESH,
                    ).start()

            def local():
                for src, dst, sem in moves:
                    pltpu.make_async_copy(src.at[:, cols], dst, sem).start()

            if step == 0:
                pl.when(at_home)(local)
                pl.when(jnp.logical_not(at_home))(remote)
            else:
                remote()

    def bias_copy(step):
        place = lax.rem(y + step, 4)
        return pltpu.make_async_remote_copy(
            src_ref=bias_own,
            dst_ref=bias.at[uly],
            send_sem=bias_send.at[step],
            recv_sem=bias_recv,
            device_id=group_device(place),
            device_id_type=MESH,
        )

    def slot_copy(j, src, dst, sems, ctx_to, uly_to):
        return pltpu.make_async_remote_copy(
            src_ref=keyval.at[j, src],
            dst_ref=keyval.at[j, dst],
            send_sem=sems.at[j],
            recv_sem=kv_recv.at[j, dst],
            device_id=(ctx_to, uly_to),
            device_id_type=MESH,
        )

    def wait_slot(j, slot):
        pltpu.make_async_copy(keyval.at[j, slot], keyval.at[j, slot], kv_recv.at[j, slot]).wait()

    def work(j, slot):
        attend(
            query, keyval, bias, st_max.at[j], st_sum.at[j], st_lin.at[j], acc_w.at[j], acc_p.at[j], j, slot
        )

    def send_out(j):
        cols = pl.ds(pl.multiple_of((y * LOCAL_HEADS + j) * HEAD, HEAD), HEAD)
        for t in range(QT):
            def remote():
                for a, out in enumerate((out_p, out_t)):
                    pltpu.make_async_remote_copy(
                        src_ref=outbuf.at[j, a, pl.ds(t * TILE, TILE), :],
                        dst_ref=out.at[:, cols],
                        send_sem=out_send.at[t, a],
                        recv_sem=out_recv.at[a],
                        device_id=(base + core, t),
                        device_id_type=MESH,
                    ).start()

            def local():
                for a, out in enumerate((out_p, out_t)):
                    pltpu.make_async_copy(
                        outbuf.at[j, a, pl.ds(t * TILE, TILE), :], out.at[:, cols], out_recv.at[a]
                    ).start()

            here = at_home & (uly == t)
            pl.when(here)(local)
            pl.when(jnp.logical_not(here))(remote)

    send_in(0)
    for step in range(4):
        if step == 0:
            @pl.when(at_home)
            def _():
                pltpu.make_async_copy(bias_own, bias.at[uly], bias_recv).start()

            @pl.when(jnp.logical_not(at_home))
            def _():
                bias_copy(0).start()
        else:
            bias_copy(step).start()
    send_in(1)

    @pl.loop(0, LOCAL_HEADS + 2)
    def _(r):
        @pl.when(r < LOCAL_HEADS)
        def _():
            j = r
            wait_slot(j, 0)
            slot_copy(j, 0, 2, z1_send, ahead, uly).start()

            @pl.when(core == 0)
            def _():
                slot_copy(j, 0, 1, xa_send, ctx, other).start()

            @pl.when(j + 2 < LOCAL_HEADS)
            def _():
                send_in(j + 2)

            @pl.when(j == 0)
            def _():
                pltpu.make_async_copy(bias, bias, bias_recv).wait()

            st_max[j] = jnp.full((CT, HEAD), NEG, jnp.float32)
            st_sum[j] = jnp.zeros((CT, HEAD), jnp.float32)
            st_lin[j] = jnp.zeros((CT, HEAD), jnp.float32)
            acc_w[j] = jnp.zeros((CT, 2 * HEAD), jnp.float32)
            acc_p[j] = jnp.zeros((CT, HEAD), jnp.float32)
            pltpu.make_async_copy(query.at[j], query.at[j], q_recv.at[j]).wait()
            work(j, 0)

        @pl.when((r >= 1) & (r < LOCAL_HEADS + 1))
        def _():
            j = r - 1
            wait_slot(j, 2)

            @pl.when(core == 0)
            def _():
                slot_copy(j, 2, 3, xb_send, ctx, other).start()

            @pl.when(core == 1)
            def _():
                slot_copy(j, 2, 3, z2_send, ahead, other).start()
                slot_copy(j, 2, 1, xb_send, ctx, other).start()

            work(j, 2)
            wait_slot(j, 1)
            work(j, 1)

        @pl.when(r >= 2)
        def _():
            j = r - 2
            wait_slot(j, 3)
            work(j, 3)
            inverse = 1.0 / st_sum[j]
            primal = acc_w[j, :, :HEAD] * inverse
            tangent = (
                SCALING * acc_p[j] + acc_w[j, :, HEAD:] - (SCALING * st_lin[j]) * primal
            ) * inverse
            outbuf[j, 0] = primal.astype(jnp.bfloat16)
            outbuf[j, 1] = tangent.astype(jnp.bfloat16)
            send_out(j)

    sources = (k_ref, kt_ref, v_ref, vt_ref, q_ref, qt_ref)
    group = pl.ds(0, LOCAL_HEADS * HEAD)
    for step in range(4):
        def sent():
            for a, src in enumerate(sources):
                pltpu.make_async_copy(src.at[:, group], src.at[:, group], in_send.at[step, a]).wait()
            bias_copy(step).wait_send()

        if step == 0:
            pl.when(jnp.logical_not(at_home))(sent)
        else:
            sent()

    @pl.loop(0, LOCAL_HEADS)
    def _(j):
        slot_copy(j, 0, 2, z1_send, ahead, uly).wait_send()
        slot_copy(j, 2, 3, xb_send, ctx, other).wait_send()

        @pl.when(core == 0)
        def _():
            slot_copy(j, 0, 1, xa_send, ctx, other).wait_send()

        @pl.when(core == 1)
        def _():
            slot_copy(j, 2, 3, z2_send, ahead, other).wait_send()

    for t in range(QT):
        @pl.when(jnp.logical_not(at_home & (uly == t)))
        def _():
            for a, out in enumerate((out_p, out_t)):
                pltpu.make_async_copy(out.at[:, group], out.at[:, group], out_send.at[t, a]).wait()

    pltpu.make_async_copy(out_p, out_p, out_recv.at[0]).wait()
    pltpu.make_async_copy(out_t, out_t, out_recv.at[1]).wait()


def on_device(n_ctx, query_rows, key_rows, value_rows, query_tan, key_tan, value_tan, tile_query, tile_key, tile_count):
    heads = LOCAL_HEADS
    anyspace = pl.BlockSpec(memory_space=pl.ANY)
    vmem = pl.BlockSpec(memory_space=pltpu.VMEM)
    dma = pltpu.SemaphoreType.DMA
    return pl.pallas_call(
        functools.partial(kernel, n_ctx),
        out_shape=(
            jax.ShapeDtypeStruct(query_rows.shape, jnp.bfloat16),
            jax.ShapeDtypeStruct(query_rows.shape, jnp.bfloat16),
        ),
        in_specs=[anyspace] * 6 + [vmem, vmem, pl.BlockSpec(memory_space=pltpu.SMEM)],
        out_specs=(anyspace, anyspace),
        scratch_shapes=[
            pltpu.VMEM((heads, CT, 2 * HEAD), jnp.bfloat16),
            pltpu.VMEM((heads, REACH, 2, CT, 2 * HEAD), jnp.bfloat16),
            pltpu.VMEM((REACH, QT, 8, HEAD), jnp.float32),
            pltpu.VMEM((QT, REACH, QT, 8, HEAD), jnp.float32),
            pltpu.VMEM((heads, CT, HEAD), jnp.float32),
            pltpu.VMEM((heads, CT, HEAD), jnp.float32),
            pltpu.VMEM((heads, CT, HEAD), jnp.float32),
            pltpu.VMEM((heads, CT, 2 * HEAD), jnp.float32),
            pltpu.VMEM((heads, CT, HEAD), jnp.float32),
            pltpu.VMEM((heads, 2, CT, HEAD), jnp.bfloat16),
            dma((4, 6)),
            dma((heads,)),
            dma((heads, REACH)),
            dma((heads,)),
            dma((heads,)),
            dma((heads,)),
            dma((heads,)),
            dma((4,)),
            dma,
            dma((QT, 2)),
            dma((2,)),
        ],
        compiler_params=pltpu.CompilerParams(
            collective_id=0, has_side_effects=True, vmem_limit_bytes=48 * 1024 * 1024
        ),
        cost_estimate=pl.CostEstimate(
            flops=heads * CT * CT * REACH * HEAD * 12,
            bytes_accessed=12 * TILE * 2560,
            transcendentals=heads * CT * CT * REACH,
        ),
        name="band_attention",
    )(query_rows, key_rows, value_rows, query_tan, key_tan, value_tan, tile_query, tile_key, tile_count)


def solution(mesh):
    rows = P(("ctx", "uly"), None)
    return jax.shard_map(
        functools.partial(on_device, mesh.shape["ctx"]),
        mesh=mesh,
        in_specs=(rows,) * 6 + (P("ctx", None), P("ctx", None), P("ctx")),
        out_specs=(rows, rows),
        check_vma=False,
    )
```

time: 372 us -> 123 us (0.33); the launches traced: 365 us -> 123 us
  waiting for transfers between devices: 160 us -> 0 us
  Pallas kernels: 0 us -> 113 us
  blocking collectives: 87.6 us -> 0 us
  matrix products: 51.3 us -> 0 us
  local copies, waits for them, and re-layouts: 57.1 us -> 8.2 us
  other arithmetic: 5.48 us -> 0 us
    ppermute x3 -> x0, waiting for transfers between devices: 160 us -> none  [shifted(): return lax.ppermute(block, axis, route)]
    pallas_call x0 -> x1, Pallas kernels: none -> 113 us  [on_device(): pl.pallas_call(functools.partial(kernel, n_ctx), out_shape=(jax.ShapeDtyp...]
    all_to_all x2 -> x0, blocking collectives: 87.6 us -> none  [the longest x1 65.5 us: on_device(): lax.all_to_all(stacked, 'uly', split_axis=2, concat_axis=1, tiled=True)]
    dot_general x24 -> x0, matrix products: 51.3 us -> none  [the longest x4 18.6 us: absorb(): jnp.einsum('qhd,khd->hqk', tan_queries, keys_here, preferred_element_type...]
    slice x14 -> x0, local copies, waits for them, and re-layouts: 20.5 us -> none  [the longest x4 12.5 us: absorb(): tan_values = band_block[3].reshape(block_rows, local_heads, HEAD)]
    another operation x8 -> x0, local copies, waits for them, and re-layouts: 15.3 us -> none  [the longest x2 8.65 us: on_device(): jnp.stack([query_rows, query_tan, key_rows, value_rows, key_tan, value_tan])]
    unnamed x91 -> x18, local copies, waits for them, and re-layouts: 16.1 us -> 8.2 us
    reduce_sum x2 -> x0, other arithmetic: 5.08 us -> none  [absorb(): weight_sum = weight_sum * rescale + jnp.sum(weights, axis=2)]
  transfers between devices with their start and end apart: 3 -> 0, of which waited for: 3 -> 0; matrix products, arithmetic and copies ran while one was open for 8% -> 0% of each run, Pallas kernels for 0% -> 0%
where the time goes in v1:
time: 123 us
  Pallas kernels  113 us (92%)
  local copies, waits for them, and re-layouts  8.2 us (7%)
  between operations  1.35 us (1%)
    pallas_call x1, Pallas kernels, on_device(): pl.pallas_call(functools.partial(kernel, n_ctx), out_shape=(jax.ShapeDtyp...  113 us
    unnamed x18, local copies, waits for them, and re-layouts  8.2 us

profile of v1, /device:TPU:1, one launch (start us, length us, event | category | flops | bytes accessed | tf_op | source)
XLA Modules:
  0.0 122.9 jit_solution(17777587183744068539)
XLA Ops:
  0.6 0.0 copy-start.7
  0.6 0.0 copy-start.6
  1.3 0.0 copy-done.7
  1.3 0.0 copy-done.6
  1.3 0.0 copy-start
  1.3 1.1 copy-done
  2.4 0.0 copy-start.1
  2.4 1.1 copy-done.1
  3.5 0.0 copy-start.2
  3.5 1.1 copy-done.2
  4.6 0.0 copy-start.3
  4.6 1.1 copy-done.3
  5.7 0.0 copy-start.4
  5.7 1.1 copy-done.4
  6.8 0.0 copy-start.5
  6.8 1.1 copy-done.5
  7.9 113.3 %band_attention.1 = (bf16[128,2560]{1,0:T(8,128)(2,1)S(1)}, bf16[128,2560]{1,0:T(8,128)(2,1)S(1)}) custom-call(bf16[128,2560]{1,0:T(8,128)(2,1)S(1)} %copy-done, bf16[128,2560]{1,0:T(8,128)(2,1)S(1)} %copy-done.1, bf16[128,2560]{1,0:T(8,128)(2,1)S(1)} %copy-done.2, bf16[128,2560]{1,0:T(8,128)(2,1)S(1)} %copy-done.3, bf16[128,2560]{1,0:T(8,128)(2,1)S(1)} %copy-done.4, ...), custom_call_target="tpu_custom_call" | custom-call | flops 8053063680 | bytes 3932160 | tf_op jit(solution)/shard_map/band_attention/pallas_call | solution.py:334
  121.2 0.8 copy.14
  122.0 0.8 copy.15
Async XLA Ops:
  0.6 0.7 copy-start.7
  0.6 0.7 copy-start.6
  1.3 1.1 copy-start
  2.4 1.1 copy-start.1
  3.5 1.1 copy-start.2
  4.6 1.1 copy-start.3
  5.7 1.1 copy-start.4
  6.8 1.1 copy-start.5

commit v2 on v1

v2 whole, which is shorter than its diff:
```python
import functools
import math
import jax
import jax.numpy as jnp
from jax import lax
from jax.experimental import pallas as pl
from jax.experimental.pallas import tpu as pltpu
from jax.sharding import PartitionSpec as P

HEAD = 128
TILE = 128
REACH = 4
MAXT = 64
LOCAL_HEADS = 5
CT = 512
QT = 4
PART = 256
MESH = pl.DeviceIdType.MESH
SCALING = HEAD ** (-0.5)
LOG2E = math.log2(math.e)
NEG = -1e30


SEND_EVEN = [0, 8, 4, 3, 11, 12, 1, 9, 2, 10]
SEND_ODD = [3, 0, 8, 12, 11, 4, 2, 1, 9, 10]
PLAN_EVEN = [0, 8, 16, 24, 4, 3, 48, 12, 40, 32, 56, 19, 11, 27, 20, 28, 44, 1, 60, 51, 43, 35, 59, 9, 52, 17, 36, 2, 49, 25, 10, 18, 41, 64, 68, 33, 57, 34, 50, 67, 42, 65, 58, 26, 66]
PLAN_ODD = [0, 16, 8, 48, 32, 40, 56, 20, 52, 19, 3, 36, 51, 4, 28, 11, 24, 43, 35, 1, 59, 12, 44, 60, 17, 9, 27, 49, 2, 41, 67, 18, 64, 57, 33, 25, 68, 10, 50, 26, 65, 42, 58, 34, 66]


def look_up(table, at):
    words = [sum(v << (7 * n) for n, v in enumerate(table[w : w + 4])) for w in range(0, len(table), 4)]
    place = at // 4
    word = jnp.int32(words[0])
    for w in range(1, len(words)):
        word = jnp.where(place == w, jnp.int32(words[w]), word)
    return lax.shift_right_logical(word, (at % 4) * 7) % 128


def attend(query, keyval, values_t, bias, j, slot, sink, stats):
    per = PART // TILE
    nt = (((1,), (1,)), ((), ()))
    for h in range(CT // PART):
        cols = pl.ds(h * PART, PART)
        scores = lax.dot_general(
            keyval[j, 0, :, :HEAD], query[j, slot, cols, HEAD:], nt, preferred_element_type=jnp.float32
        )
        tans = lax.dot_general(
            keyval[j, 0], query[j, slot, cols, :], nt, preferred_element_type=jnp.float32
        )
        masked = []
        for c in range(QT):
            wide = jnp.concatenate([bias[slot, h * per + t, c] for t in range(per)], axis=1)
            masked.extend([wide] * (TILE // 8))
        scores = scores * (SCALING * LOG2E) + jnp.concatenate(masked, axis=0)
        top = jnp.max(scores, axis=0, keepdims=True)
        weights = jnp.exp2(scores - top)
        product = weights * tans
        total = jnp.sum(weights, axis=0, keepdims=True)
        inverse = 1.0 / total
        mean_tan = SCALING * jnp.sum(product, axis=0, keepdims=True) * inverse
        by_weight = jnp.dot(values_t[j], weights.astype(jnp.bfloat16), preferred_element_type=jnp.float32)
        by_product = jnp.dot(
            values_t[j, :HEAD, :], product.astype(jnp.bfloat16), preferred_element_type=jnp.float32
        )
        primal = by_weight[:HEAD] * inverse
        tangent = (SCALING * by_product + by_weight[HEAD:]) * inverse - mean_tan * primal
        sink[0, :, cols] = primal.astype(sink.dtype)
        sink[1, :, cols] = tangent.astype(sink.dtype)
        stats[0:1, cols] = top
        stats[1:2, cols] = total
        stats[2:3, cols] = mean_tan


def merge(own, own_stats, came, came_stats, sink):
    for h in range(CT // PART):
        cols = pl.ds(h * PART, PART)
        top_a, top_b = own_stats[0:1, cols], came_stats[0:1, cols]
        tan_a, tan_b = own_stats[2:3, cols], came_stats[2:3, cols]
        top = jnp.maximum(top_a, top_b)
        part_a = own_stats[1:2, cols] * jnp.exp2(top_a - top)
        part_b = came_stats[1:2, cols] * jnp.exp2(top_b - top)
        total = part_a + part_b
        inverse = 1.0 / total
        part_a, part_b = part_a * inverse, part_b * inverse
        mean_tan = part_a * tan_a + part_b * tan_b
        primal_a, primal_b = own[0, :, cols], came[0, :, cols].astype(jnp.float32)
        tangent_a, tangent_b = own[1, :, cols], came[1, :, cols].astype(jnp.float32)
        primal = part_a * primal_a + part_b * primal_b
        tangent = part_a * (tangent_a + (tan_a - mean_tan) * primal_a) + part_b * (
            tangent_b + (tan_b - mean_tan) * primal_b
        )
        sink[0, :, cols] = primal.astype(sink.dtype)
        sink[1, :, cols] = tangent.astype(sink.dtype)
        own_stats[0:1, cols] = top
        own_stats[1:2, cols] = total
        own_stats[2:3, cols] = mean_tan


def kernel(
    n_ctx,
    q_ref,
    k_ref,
    v_ref,
    qt_ref,
    kt_ref,
    vt_ref,
    tq_ref,
    tk_ref,
    cnt_ref,
    out_p,
    out_t,
    query,
    keyval,
    values_t,
    bias_own,
    bias_rows,
    bias,
    local,
    local_stats,
    sent,
    sent_stats,
    came,
    came_stats,
    outbuf,
    in_send,
    q_recv,
    kv_recv,
    zq_send,
    xq_send,
    fq_send,
    bias_send,
    bias_hop_send,
    bias_recv,
    part_send,
    part_recv,
    stat_send,
    stat_recv,
    out_send,
    out_recv,
):
    ctx = lax.axis_index("ctx")
    uly = lax.axis_index("uly")
    core = lax.rem(uly, 2)
    yh = lax.rem(ctx, 2)
    base = ctx - yh
    y = yh * 2 + lax.div(uly, 2)
    other = uly + 1 - 2 * core
    ahead = lax.rem(ctx + 2, n_ctx)
    behind = lax.rem(ctx + n_ctx - 2, n_ctx)
    behind_or_here = lax.rem(ctx + (1 - core) * (n_ctx - 2), n_ctx)
    here_or_ahead = lax.rem(ctx + core * 2, n_ctx)
    at_home = core == yh

    barrier = pltpu.get_barrier_semaphore()
    for step in range(1, 8):
        place = lax.rem(yh * 4 + uly + step, 8)
        pl.semaphore_signal(
            barrier, inc=1, device_id=(base + lax.div(place, 4), lax.rem(place, 4)), device_id_type=MESH
        )
    for where in (ahead, behind):
        for who in (uly, other):
            pl.semaphore_signal(barrier, inc=1, device_id=(where, who), device_id_type=MESH)

    lane = lax.broadcasted_iota(jnp.int32, (REACH * QT, MAXT), 1)
    code = lax.broadcasted_iota(jnp.int32, (REACH * QT, MAXT), 0)
    row = lax.broadcasted_iota(jnp.int32, (REACH * QT, 1), 0)
    usable = (lane < cnt_ref[0]) & (jnp.broadcast_to(tq_ref[...], code.shape) == uly)
    hit = usable & (jnp.broadcast_to(tk_ref[...], code.shape) == code)
    seen = jnp.max(jnp.where(hit, 1.0, 0.0), axis=1, keepdims=True)
    seen = jnp.maximum(seen, jnp.where(row == uly, 1.0, 0.0))
    bias_own[...] = jnp.broadcast_to((1.0 - seen) * NEG, (REACH * QT, HEAD))

    pl.semaphore_wait(barrier, 11)

    own_rows = pl.ds(pl.multiple_of(uly * TILE, TILE), TILE)
    low_half, high_half = pl.ds(0, HEAD), pl.ds(HEAD, HEAD)

    def group_device(place):
        return (base + lax.div(place, 2), lax.rem(place, 2) * 2 + yh)

    def send_in(moves, first, j):
        for step in range(4):
            place = lax.rem(y + step, 4)
            cols = pl.ds(pl.multiple_of((place * LOCAL_HEADS + j) * HEAD, HEAD), HEAD)

            def remote():
                for a, (src, dst, sem) in enumerate(moves):
                    pltpu.make_async_remote_copy(
                        src_ref=src.at[:, cols],
                        dst_ref=dst,
                        send_sem=in_send.at[step, first + a],
                        recv_sem=sem,
                        device_id=group_device(place),
                        device_id_type=MESH,
                    ).start()

            def stay():
                for src, dst, sem in moves:
                    pltpu.make_async_copy(src.at[:, cols], dst, sem).start()

            if step == 0:
                pl.when(at_home)(stay)
                pl.when(jnp.logical_not(at_home))(remote)
            else:
                remote()

    def send_q(j):
        send_in(
            (
                (q_ref, query.at[j, 0, own_rows, high_half], q_recv.at[j, 0]),
                (qt_ref, query.at[j, 0, own_rows, low_half], q_recv.at[j, 0]),
            ),
            0,
            j,
        )

    def send_kv(j):
        send_in(
            (
                (k_ref, keyval.at[j, 0, own_rows, low_half], kv_recv.at[j]),
                (kt_ref, keyval.at[j, 0, own_rows, high_half], kv_recv.at[j]),
                (v_ref, keyval.at[j, 1, own_rows, low_half], kv_recv.at[j]),
                (vt_ref, keyval.at[j, 1, own_rows, high_half], kv_recv.at[j]),
            ),
            2,
            j,
        )

    def bias_copy(step):
        return pltpu.make_async_remote_copy(
            src_ref=bias_own,
            dst_ref=bias_rows.at[0, uly],
            send_sem=bias_send.at[step],
            recv_sem=bias_recv.at[0],
            device_id=group_device(lax.rem(y + step, 4)),
            device_id_type=MESH,
        )

    def hop(j, src, dst, sems, ctx_to, uly_to):
        return pltpu.make_async_remote_copy(
            src_ref=query.at[j, src],
            dst_ref=query.at[j, dst],
            send_sem=sems.at[j],
            recv_sem=q_recv.at[j, dst],
            device_id=(ctx_to, uly_to),
            device_id_type=MESH,
        )

    def bias_hop(src, dst, way, ctx_to, uly_to):
        return pltpu.make_async_remote_copy(
            src_ref=bias_rows.at[src],
            dst_ref=bias_rows.at[dst],
            send_sem=bias_hop_send.at[way],
            recv_sem=bias_recv.at[dst],
            device_id=(ctx_to, uly_to),
            device_id_type=MESH,
        )

    def wait_query(j, slot):
        pltpu.make_async_copy(query.at[j, slot], query.at[j, slot], q_recv.at[j, slot]).wait()

    def wait_bias(slot):
        pltpu.make_async_copy(bias_rows.at[slot], bias_rows.at[slot], bias_recv.at[slot]).wait()

    def spread_bias(slot):
        for t in range(QT):
            for c in range(QT):
                at = slot * QT + c
                bias[slot, t, c] = jnp.broadcast_to(bias_rows[slot, t, at : at + 1, :], (8, HEAD))

    def forward_own(j):
        wait_query(j, 0)
        hop(j, 0, 2, zq_send, behind, uly).start()

        @pl.when(core == 1)
        def _():
            hop(j, 0, 1, xq_send, ctx, other).start()

        @pl.when(j == 0)
        def _():
            wait_bias(0)
            bias_hop(0, 2, 0, behind, uly).start()

            @pl.when(core == 1)
            def _():
                bias_hop(0, 1, 1, ctx, other).start()

            spread_bias(0)

    def forward_next(j):
        wait_query(j, 2)
        hop(j, 2, 3, fq_send, behind_or_here, other).start()

        @pl.when(core == 0)
        def _():
            hop(j, 2, 1, xq_send, ctx, other).start()

        @pl.when(j == 0)
        def _():
            wait_bias(2)
            bias_hop(2, 3, 2, behind_or_here, other).start()

            @pl.when(core == 0)
            def _():
                bias_hop(2, 1, 1, ctx, other).start()

            spread_bias(2)

    def part_copies(j, src, dst, ctx_to, uly_to):
        return [
            pltpu.make_async_remote_copy(
                src_ref=a.at[j, src],
                dst_ref=b.at[j, dst],
                send_sem=ss.at[j, src],
                recv_sem=rs.at[j, dst],
                device_id=(ctx_to, uly_to),
                device_id_type=MESH,
            )
            for a, b, ss, rs in (
                (sent, came, part_send, part_recv),
                (sent_stats, came_stats, stat_send, stat_recv),
            )
        ]

    def start_part(*args):
        for copy in part_copies(*args):
            copy.start()

    def wait_part(j, dst):
        pltpu.make_async_copy(came.at[j, dst], came.at[j, dst], part_recv.at[j, dst]).wait()
        pltpu.make_async_copy(came_stats.at[j, dst], came_stats.at[j, dst], stat_recv.at[j, dst]).wait()

    def work(j, slot):
        if slot % 2 == 0:
            sink, stats = local.at[j, slot // 2], local_stats.at[j, slot // 2]
        else:
            sink, stats = sent.at[j, slot // 2], sent_stats.at[j, slot // 2]
        attend(query, keyval, values_t, bias, j, slot, sink, stats)

    def absorb(j, which, dst, sink):
        merge(local.at[j, which], local_stats.at[j, which], came.at[j, dst], came_stats.at[j, dst], sink)

    def send_out(j):
        cols = pl.ds(pl.multiple_of((y * LOCAL_HEADS + j) * HEAD, HEAD), HEAD)
        for t in range(QT):
            def remote():
                for a, out in enumerate((out_p, out_t)):
                    pltpu.make_async_remote_copy(
                        src_ref=outbuf.at[j, a, pl.ds(t * TILE, TILE), :],
                        dst_ref=out.at[:, cols],
                        send_sem=out_send.at[t, a],
                        recv_sem=out_recv.at[a],
                        device_id=(base + core, t),
                        device_id_type=MESH,
                    ).start()

            def stay():
                for a, out in enumerate((out_p, out_t)):
                    pltpu.make_async_copy(
                        outbuf.at[j, a, pl.ds(t * TILE, TILE), :], out.at[:, cols], out_recv.at[a]
                    ).start()

            here = at_home & (uly == t)
            pl.when(here)(stay)
            pl.when(jnp.logical_not(here))(remote)

    @pl.when(at_home)
    def _():
        pltpu.make_async_copy(bias_own, bias_rows.at[0, uly], bias_recv.at[0]).start()

    @pl.when(jnp.logical_not(at_home))
    def _():
        bias_copy(0).start()

    for step in range(1, 4):
        bias_copy(step).start()
    def take_kv(j):
        pltpu.make_async_copy(keyval.at[j], keyval.at[j], kv_recv.at[j]).wait()
        values_t[j] = keyval[j, 1].T

    def work_from(j, slot):
        wait_query(j, slot)

        @pl.when(j == 0)
        def _():
            wait_bias(slot)
            spread_bias(slot)

        work(j, slot)

    @pl.loop(0, 2 * LOCAL_HEADS)
    def _(at):
        item = jnp.where(yh == 0, look_up(SEND_EVEN, at), look_up(SEND_ODD, at))
        j = item % 8
        pl.when(item < 8)(lambda: send_q(j))
        pl.when(item >= 8)(lambda: send_kv(j))

    @pl.loop(0, len(PLAN_EVEN))
    def _(at):
        item = jnp.where(core == 0, look_up(PLAN_EVEN, at), look_up(PLAN_ODD, at))
        j, what = item % 8, item // 8

        def attend_pass_previous():
            work_from(j, 1)
            start_part(j, 0, 1 - core, ctx, other)

        def attend_pass_far():
            work_from(j, 3)
            start_part(j, 1, core, here_or_ahead, other)

        def pass_on():
            @pl.when(core == 0)
            def _():
                wait_part(j, 1)
                absorb(j, 1, 1, local.at[j, 1])

            wait_part(j, 0)
            absorb(j, 1, 0, sent.at[j, 2])
            sent_stats[j, 2] = local_stats[j, 1]
            start_part(j, 2, 2, ahead, uly)

        def finish():
            @pl.when(core == 1)
            def _():
                wait_part(j, 1)
                absorb(j, 0, 1, local.at[j, 0])

            wait_part(j, 2)
            absorb(j, 0, 2, local.at[j, 0])
            outbuf[j, 0] = local[j, 0, 0].T.astype(jnp.bfloat16)
            outbuf[j, 1] = local[j, 0, 1].T.astype(jnp.bfloat16)
            send_out(j)

        steps = (
            lambda: forward_own(j),
            lambda: forward_next(j),
            lambda: take_kv(j),
            lambda: work(j, 0),
            attend_pass_previous,
            lambda: work(j, 2),
            attend_pass_far,
            pass_on,
            finish,
        )
        for number, step in enumerate(steps):
            pl.when(what == number)(step)

    group = pl.ds(0, LOCAL_HEADS * HEAD)
    for step in range(4):
        def gone():
            for a, src in enumerate((q_ref, qt_ref, k_ref, kt_ref, v_ref, vt_ref)):
                pltpu.make_async_copy(src.at[:, group], src.at[:, group], in_send.at[step, a]).wait()
            bias_copy(step).wait_send()

        if step == 0:
            pl.when(jnp.logical_not(at_home))(gone)
        else:
            gone()

    bias_hop(0, 2, 0, behind, uly).wait_send()
    bias_hop(0, 1, 1, ctx, other).wait_send()
    bias_hop(2, 3, 2, behind_or_here, other).wait_send()

    @pl.loop(0, LOCAL_HEADS)
    def _(j):
        hop(j, 0, 2, zq_send, behind, uly).wait_send()
        hop(j, 0, 1, xq_send, ctx, other).wait_send()
        hop(j, 2, 3, fq_send, behind_or_here, other).wait_send()
        for copy in (
            part_copies(j, 0, 1 - core, ctx, other)
            + part_copies(j, 1, core, here_or_ahead, other)
            + part_copies(j, 2, 2, ahead, uly)
        ):
            copy.wait_send()

    for t in range(QT):
        @pl.when(jnp.logical_not(at_home & (uly == t)))
        def _():
            for a, out in enumerate((out_p, out_t)):
                pltpu.make_async_copy(out.at[:, group], out.at[:, group], out_send.at[t, a]).wait()

    pltpu.make_async_copy(out_p, out_p, out_recv.at[0]).wait()
    pltpu.make_async_copy(out_t, out_t, out_recv.at[1]).wait()


def on_device(n_ctx, query_rows, key_rows, value_rows, query_tan, key_tan, value_tan, tile_query, tile_key, tile_count):
    heads = LOCAL_HEADS
    anyspace = pl.BlockSpec(memory_space=pl.ANY)
    vmem = pl.BlockSpec(memory_space=pltpu.VMEM)
    dma = pltpu.SemaphoreType.DMA
    return pl.pallas_call(
        functools.partial(kernel, n_ctx),
        out_shape=(
            jax.ShapeDtypeStruct(query_rows.shape, jnp.bfloat16),
            jax.ShapeDtypeStruct(query_rows.shape, jnp.bfloat16),
        ),
        in_specs=[anyspace] * 6 + [vmem, vmem, pl.BlockSpec(memory_space=pltpu.SMEM)],
        out_specs=(anyspace, anyspace),
        scratch_shapes=[
            pltpu.VMEM((heads, REACH, CT, 2 * HEAD), jnp.bfloat16),
            pltpu.VMEM((heads, 2, CT, 2 * HEAD), jnp.bfloat16),
            pltpu.VMEM((heads, 2 * HEAD, CT), jnp.bfloat16),
            pltpu.VMEM((REACH * QT, HEAD), jnp.float32),
            pltpu.VMEM((REACH, QT, REACH * QT, HEAD), jnp.float32),
            pltpu.VMEM((REACH, QT, QT, 8, HEAD), jnp.float32),
            pltpu.VMEM((heads, 2, 2, HEAD, CT), jnp.float32),
            pltpu.VMEM((heads, 2, 8, CT), jnp.float32),
            pltpu.VMEM((heads, 3, 2, HEAD, CT), jnp.bfloat16),
            pltpu.VMEM((heads, 3, 8, CT), jnp.float32),
            pltpu.VMEM((heads, 3, 2, HEAD, CT), jnp.bfloat16),
            pltpu.VMEM((heads, 3, 8, CT), jnp.float32),
            pltpu.VMEM((heads, 2, CT, HEAD), jnp.bfloat16),
            dma((4, 6)),
            dma((heads, REACH)),
            dma((heads,)),
            dma((heads,)),
            dma((heads,)),
            dma((heads,)),
            dma((4,)),
            dma((3,)),
            dma((REACH,)),
            dma((heads, 3)),
            dma((heads, 3)),
            dma((heads, 3)),
            dma((heads, 3)),
            dma((QT, 2)),
            dma((2,)),
        ],
        compiler_params=pltpu.CompilerParams(
            collective_id=0, has_side_effects=True, vmem_limit_bytes=60 * 1024 * 1024
        ),
        cost_estimate=pl.CostEstimate(
            flops=heads * CT * CT * REACH * HEAD * 12,
            bytes_accessed=12 * TILE * 2560,
            transcendentals=heads * CT * CT * REACH,
        ),
        name="band_attention",
    )(query_rows, key_rows, value_rows, query_tan, key_tan, value_tan, tile_query, tile_key, tile_count)


def solution(mesh):
    rows = P(("ctx", "uly"), None)
    return jax.shard_map(
        functools.partial(on_device, mesh.shape["ctx"]),
        mesh=mesh,
        in_specs=(rows,) * 6 + (P("ctx", None), P("ctx", None), P("ctx")),
        out_specs=(rows, rows),
        check_vma=False,
    )
```

time: 123 us -> 98.1 us (0.80)
  Pallas kernels: 113 us -> 93.8 us
  local copies, waits for them, and re-layouts: 8.2 us -> 2.87 us
    pallas_call x1, Pallas kernels: 113 us -> 93.8 us  [on_device(): pl.pallas_call(functools.partial(kernel, n_ctx), out_shape=(jax.ShapeDtyp...]
    unnamed x18 -> x4, local copies, waits for them, and re-layouts: 8.2 us -> 2.87 us
where the time goes in v2:
time: 98.1 us; the launch traced here: 98 us
  Pallas kernels  93.8 us (96%)
  local copies, waits for them, and re-layouts  2.87 us (3%)
  between operations  1.3 us (1%)
    pallas_call x1, Pallas kernels, on_device(): pl.pallas_call(functools.partial(kernel, n_ctx), out_shape=(jax.ShapeDtyp...  93.8 us
    unnamed x4, local copies, waits for them, and re-layouts  2.87 us

profile of v2, /device:TPU:1, one launch (start us, length us, event | category | flops | bytes accessed | tf_op | source)
XLA Modules:
  0.0 98.0 jit_solution(3634252683106099063)
XLA Ops:
  1.3 93.8 %band_attention.1 = (bf16[128,2560]{1,0:T(8,128)(2,1)}, bf16[128,2560]{1,0:T(8,128)(2,1)}) custom-call(bf16[128,2560]{1,0:T(8,128)(2,1)} %q_ref.1, bf16[128,2560]{1,0:T(8,128)(2,1)} %k_ref.1, bf16[128,2560]{1,0:T(8,128)(2,1)} %v_ref.1, bf16[128,2560]{1,0:T(8,128)(2,1)} %qt_ref.1, bf16[128,2560]{1,0:T(8,128)(2,1)} %kt_ref.1, bf16[128,2560]{1,0:T(8,128)(2,1)} %vt_ref.1, ...), custom_call_target="tpu_custom_call" | custom-call | flops 8053063680 | bytes 3932160 | tf_op jit(solution)/shard_map/band_attention/pallas_call | solution.py:491
  95.1 0.0 copy-start
  95.1 2.0 %copy.14 = bf16[128,2560]{1,0:T(8,128)(2,1)} copy(bf16[128,2560]{1,0:T(8,128)(2,1)} %get-tuple-element.4) | data formatting | bytes 1310720
  97.2 0.0 copy-done
  97.2 0.8 copy.15
Async XLA Ops:
  95.1 2.0 %copy-start = (bf16[128,2560]{1,0:T(8,128)(2,1)S(1)}, bf16[128,2560]{1,0:T(8,128)(2,1)}, u32[]{:S(2)}) copy-start(bf16[128,2560]{1,0:T(8,128)(2,1)} %get-tuple-element.5) | copy-start | bytes 1966084

commit v3 on v2

--- a/solution.py
+++ b/solution.py
@@ -21,10 +21,10 @@
 NEG = -1e30
 
 
-SEND_EVEN = [0, 8, 4, 3, 11, 12, 1, 9, 2, 10]
-SEND_ODD = [3, 0, 8, 12, 11, 4, 2, 1, 9, 10]
-PLAN_EVEN = [0, 8, 16, 24, 4, 3, 48, 12, 40, 32, 56, 19, 11, 27, 20, 28, 44, 1, 60, 51, 43, 35, 59, 9, 52, 17, 36, 2, 49, 25, 10, 18, 41, 64, 68, 33, 57, 34, 50, 67, 42, 65, 58, 26, 66]
-PLAN_ODD = [0, 16, 8, 48, 32, 40, 56, 20, 52, 19, 3, 36, 51, 4, 28, 11, 24, 43, 35, 1, 59, 12, 44, 60, 17, 9, 27, 49, 2, 41, 67, 18, 64, 57, 33, 25, 68, 10, 50, 26, 65, 42, 58, 34, 66]
+SEND_EVEN = [0, 8, 2, 1, 3, 4, 10, 9, 11, 12]
+SEND_ODD = [2, 0, 8, 10, 9, 11, 3, 1, 4, 12]
+PLAN_EVEN = [0, 8, 16, 2, 48, 1, 10, 40, 9, 32, 56, 24, 3, 18, 4, 50, 42, 11, 17, 58, 34, 41, 57, 12, 19, 43, 51, 26, 25, 66, 20, 49, 64, 28, 59, 35, 65, 52, 44, 33, 27, 36, 60, 67, 68]
+PLAN_ODD = [0, 16, 8, 48, 40, 24, 56, 32, 2, 18, 50, 10, 17, 49, 42, 58, 34, 33, 3, 19, 35, 26, 1, 25, 11, 51, 43, 59, 4, 9, 20, 52, 64, 66, 41, 27, 57, 12, 44, 67, 28, 60, 36, 65, 68]
 
 
 def look_up(table, at):
@@ -137,6 +137,7 @@
     stat_recv,
     out_send,
     out_recv,
+    told,
 ):
     ctx = lax.axis_index("ctx")
     uly = lax.axis_index("uly")
@@ -152,14 +153,21 @@
     at_home = core == yh
 
     barrier = pltpu.get_barrier_semaphore()
-    for step in range(1, 8):
-        place = lax.rem(yh * 4 + uly + step, 8)
-        pl.semaphore_signal(
-            barrier, inc=1, device_id=(base + lax.div(place, 4), lax.rem(place, 4)), device_id_type=MESH
-        )
+    chip = uly - core
+    for step in range(4):
+        place = lax.rem(y + step, 4)
+
+        def greet():
+            pl.semaphore_signal(
+                barrier, inc=1, device_id=(base + lax.div(place, 2), lax.rem(place, 2) * 2), device_id_type=MESH
+            )
+
+        if step == 0:
+            pl.when(core == 1)(greet)
+        else:
+            greet()
     for where in (ahead, behind):
-        for who in (uly, other):
-            pl.semaphore_signal(barrier, inc=1, device_id=(where, who), device_id_type=MESH)
+        pl.semaphore_signal(barrier, inc=1, device_id=(where, chip + 1), device_id_type=MESH)
 
     lane = lax.broadcasted_iota(jnp.int32, (REACH * QT, MAXT), 1)
     code = lax.broadcasted_iota(jnp.int32, (REACH * QT, MAXT), 0)
@@ -170,7 +178,14 @@
     seen = jnp.maximum(seen, jnp.where(row == uly, 1.0, 0.0))
     bias_own[...] = jnp.broadcast_to((1.0 - seen) * NEG, (REACH * QT, HEAD))
 
-    pl.semaphore_wait(barrier, 11)
+    @pl.when(core == 0)
+    def _():
+        pl.semaphore_wait(barrier, 7)
+        pl.semaphore_signal(told, inc=1, device_id=(ctx, other), device_id_type=MESH)
+
+    @pl.when(core == 1)
+    def _():
+        pl.semaphore_wait(told, 1)
 
     own_rows = pl.ds(pl.multiple_of(uly * TILE, TILE), TILE)
     low_half, high_half = pl.ds(0, HEAD), pl.ds(HEAD, HEAD)
@@ -395,6 +410,15 @@
         pl.when(item < 8)(lambda: send_q(j))
         pl.when(item >= 8)(lambda: send_kv(j))
 
+    @pl.when(core == 1)
+    def _():
+        pl.semaphore_wait(barrier, 4)
+        pl.semaphore_signal(told, inc=1, device_id=(ctx, other), device_id_type=MESH)
+
+    @pl.when(core == 0)
+    def _():
+        pl.semaphore_wait(told, 1)
+
     @pl.loop(0, len(PLAN_EVEN))
     def _(at):
         item = jnp.where(core == 0, look_up(PLAN_EVEN, at), look_up(PLAN_ODD, at))
@@ -486,6 +510,7 @@
 def on_device(n_ctx, query_rows, key_rows, value_rows, query_tan, key_tan, value_tan, tile_query, tile_key, tile_count):
     heads = LOCAL_HEADS
     anyspace = pl.BlockSpec(memory_space=pl.ANY)
+    hbm = pl.BlockSpec(memory_space=pltpu.HBM)
     vmem = pl.BlockSpec(memory_space=pltpu.VMEM)
     dma = pltpu.SemaphoreType.DMA
     return pl.pallas_call(
@@ -494,7 +519,7 @@
             jax.ShapeDtypeStruct(query_rows.shape, jnp.bfloat16),
             jax.ShapeDtypeStruct(query_rows.shape, jnp.bfloat16),
         ),
-        in_specs=[anyspace] * 6 + [vmem, vmem, pl.BlockSpec(memory_space=pltpu.SMEM)],
+        in_specs=[hbm] * 6 + [vmem, vmem, pl.BlockSpec(memory_space=pltpu.SMEM)],
         out_specs=(anyspace, anyspace),
         scratch_shapes=[
             pltpu.VMEM((heads, REACH, CT, 2 * HEAD), jnp.bfloat16),
@@ -525,6 +550,7 @@
             dma((heads, 3)),
             dma((QT, 2)),
             dma((2,)),
+            pltpu.SemaphoreType.REGULAR,
         ],
         compiler_params=pltpu.CompilerParams(
             collective_id=0, has_side_effects=True, vmem_limit_bytes=60 * 1024 * 1024

time: 98.1 us -> 90.7 us (0.925)
  Pallas kernels: 93.8 us -> 86.4 us
    pallas_call x1, Pallas kernels: 93.8 us -> 86.4 us  [on_device(): pl.pallas_call(functools.partial(kernel, n_ctx), out_shape=(jax.ShapeDtyp...]
where the time goes in v3:
time: 90.7 us; the launch traced here: 90.6 us
  Pallas kernels  86.4 us (95%)
  local copies, waits for them, and re-layouts  2.87 us (3%)
  between operations  1.3 us (1%)
    pallas_call x1, Pallas kernels, on_device(): pl.pallas_call(functools.partial(kernel, n_ctx), out_shape=(jax.ShapeDtyp...  86.4 us
    unnamed x4, local copies, waits for them, and re-layouts  2.87 us

profile of v3, /device:TPU:1, one launch (start us, length us, event | category | flops | bytes accessed | tf_op | source)
XLA Modules:
  0.0 90.6 jit_solution(3333315787501376460)
XLA Ops:
  1.3 86.4 %band_attention.1 = (bf16[128,2560]{1,0:T(8,128)(2,1)}, bf16[128,2560]{1,0:T(8,128)(2,1)}) custom-call(bf16[128,2560]{1,0:T(8,128)(2,1)} %q_ref.1, bf16[128,2560]{1,0:T(8,128)(2,1)} %k_ref.1, bf16[128,2560]{1,0:T(8,128)(2,1)} %v_ref.1, bf16[128,2560]{1,0:T(8,128)(2,1)} %qt_ref.1, bf16[128,2560]{1,0:T(8,128)(2,1)} %kt_ref.1, bf16[128,2560]{1,0:T(8,128)(2,1)} %vt_ref.1, ...), custom_call_target="tpu_custom_call" | custom-call | flops 8053063680 | bytes 3932160 | tf_op jit(solution)/shard_map/band_attention/pallas_call | solution.py:516
  87.7 0.0 copy-start
  87.7 2.0 %copy.14 = bf16[128,2560]{1,0:T(8,128)(2,1)} copy(bf16[128,2560]{1,0:T(8,128)(2,1)} %get-tuple-element.4) | data formatting | bytes 1310720
  89.7 0.0 copy-done
  89.7 0.8 copy.15
Async XLA Ops:
  87.7 2.0 %copy-start = (bf16[128,2560]{1,0:T(8,128)(2,1)S(1)}, bf16[128,2560]{1,0:T(8,128)(2,1)}, u32[]{:S(2)}) copy-start(bf16[128,2560]{1,0:T(8,128)(2,1)} %get-tuple-element.5) | copy-start | bytes 1966084

commit v4 on v3

--- a/solution.py
+++ b/solution.py
@@ -21,10 +21,11 @@
 NEG = -1e30
 
 
-SEND_EVEN = [0, 8, 2, 1, 3, 4, 10, 9, 11, 12]
-SEND_ODD = [2, 0, 8, 10, 9, 11, 3, 1, 4, 12]
-PLAN_EVEN = [0, 8, 16, 2, 48, 1, 10, 40, 9, 32, 56, 24, 3, 18, 4, 50, 42, 11, 17, 58, 34, 41, 57, 12, 19, 43, 51, 26, 25, 66, 20, 49, 64, 28, 59, 35, 65, 52, 44, 33, 27, 36, 60, 67, 68]
-PLAN_ODD = [0, 16, 8, 48, 40, 24, 56, 32, 2, 18, 50, 10, 17, 49, 42, 58, 34, 33, 3, 19, 35, 26, 1, 25, 11, 51, 43, 59, 4, 9, 20, 52, 64, 66, 41, 27, 57, 12, 44, 67, 28, 60, 36, 65, 68]
+MEET = [1, 0, 1, 0, 0]
+SEND_EVEN = [4, 0, 8, 2, 3, 10, 12, 1, 11, 9]
+SEND_ODD = [8, 0, 10, 12, 4, 2, 3, 11, 1, 9]
+PLAN_EVEN = [0, 16, 4, 8, 24, 2, 40, 48, 12, 3, 32, 10, 18, 72, 42, 56, 74, 58, 20, 44, 26, 11, 60, 1, 52, 36, 50, 34, 28, 64, 9, 19, 51, 66, 35, 68, 43, 59, 27, 17, 33, 49, 41, 67, 57, 25, 65]
+PLAN_ODD = [16, 48, 0, 18, 50, 8, 40, 32, 56, 20, 24, 52, 4, 2, 34, 26, 12, 3, 36, 44, 10, 42, 60, 11, 19, 43, 58, 64, 51, 28, 1, 27, 59, 35, 68, 66, 17, 49, 9, 25, 41, 67, 57, 33, 65, 80, 80]
 
 
 def look_up(table, at):
@@ -36,20 +37,20 @@
     return lax.shift_right_logical(word, (at % 4) * 7) % 128
 
 
-def attend(query, keyval, values_t, bias, j, slot, sink, stats):
+def attend(query, keys, values_t, bias, sink, stats):
     per = PART // TILE
     nt = (((1,), (1,)), ((), ()))
     for h in range(CT // PART):
         cols = pl.ds(h * PART, PART)
         scores = lax.dot_general(
-            keyval[j, 0, :, :HEAD], query[j, slot, cols, HEAD:], nt, preferred_element_type=jnp.float32
+            keys[:, :HEAD], query[cols, HEAD:], nt, preferred_element_type=jnp.float32
         )
         tans = lax.dot_general(
-            keyval[j, 0], query[j, slot, cols, :], nt, preferred_element_type=jnp.float32
+            keys[...], query[cols, :], nt, preferred_element_type=jnp.float32
         )
         masked = []
         for c in range(QT):
-            wide = jnp.concatenate([bias[slot, h * per + t, c] for t in range(per)], axis=1)
+            wide = jnp.concatenate([bias[h * per + t, c] for t in range(per)], axis=1)
             masked.extend([wide] * (TILE // 8))
         scores = scores * (SCALING * LOG2E) + jnp.concatenate(masked, axis=0)
         top = jnp.max(scores, axis=0, keepdims=True)
@@ -58,27 +59,27 @@
         total = jnp.sum(weights, axis=0, keepdims=True)
         inverse = 1.0 / total
         mean_tan = SCALING * jnp.sum(product, axis=0, keepdims=True) * inverse
-        by_weight = jnp.dot(values_t[j], weights.astype(jnp.bfloat16), preferred_element_type=jnp.float32)
+        by_weight = jnp.dot(values_t[...], weights.astype(jnp.bfloat16), preferred_element_type=jnp.float32)
         by_product = jnp.dot(
-            values_t[j, :HEAD, :], product.astype(jnp.bfloat16), preferred_element_type=jnp.float32
+            values_t[:HEAD, :], product.astype(jnp.bfloat16), preferred_element_type=jnp.float32
         )
         primal = by_weight[:HEAD] * inverse
         tangent = (SCALING * by_product + by_weight[HEAD:]) * inverse - mean_tan * primal
         sink[0, :, cols] = primal.astype(sink.dtype)
         sink[1, :, cols] = tangent.astype(sink.dtype)
-        stats[0:1, cols] = top
-        stats[1:2, cols] = total
-        stats[2:3, cols] = mean_tan
+        stats[3 * h : 3 * h + 1, :] = top
+        stats[3 * h + 1 : 3 * h + 2, :] = total
+        stats[3 * h + 2 : 3 * h + 3, :] = mean_tan
 
 
 def merge(own, own_stats, came, came_stats, sink):
     for h in range(CT // PART):
         cols = pl.ds(h * PART, PART)
-        top_a, top_b = own_stats[0:1, cols], came_stats[0:1, cols]
-        tan_a, tan_b = own_stats[2:3, cols], came_stats[2:3, cols]
+        top_a, top_b = own_stats[3 * h : 3 * h + 1, :], came_stats[3 * h : 3 * h + 1, :]
+        tan_a, tan_b = own_stats[3 * h + 2 : 3 * h + 3, :], came_stats[3 * h + 2 : 3 * h + 3, :]
         top = jnp.maximum(top_a, top_b)
-        part_a = own_stats[1:2, cols] * jnp.exp2(top_a - top)
-        part_b = came_stats[1:2, cols] * jnp.exp2(top_b - top)
+        part_a = own_stats[3 * h + 1 : 3 * h + 2, :] * jnp.exp2(top_a - top)
+        part_b = came_stats[3 * h + 1 : 3 * h + 2, :] * jnp.exp2(top_b - top)
         total = part_a + part_b
         inverse = 1.0 / total
         part_a, part_b = part_a * inverse, part_b * inverse
@@ -91,9 +92,9 @@
         )
         sink[0, :, cols] = primal.astype(sink.dtype)
         sink[1, :, cols] = tangent.astype(sink.dtype)
-        own_stats[0:1, cols] = top
-        own_stats[1:2, cols] = total
-        own_stats[2:3, cols] = mean_tan
+        own_stats[3 * h : 3 * h + 1, :] = top
+        own_stats[3 * h + 1 : 3 * h + 2, :] = total
+        own_stats[3 * h + 2 : 3 * h + 3, :] = mean_tan
 
 
 def kernel(
@@ -107,8 +108,7 @@
     tq_ref,
     tk_ref,
     cnt_ref,
-    out_p,
-    out_t,
+    out_both,
     query,
     keyval,
     values_t,
@@ -138,7 +138,12 @@
     out_send,
     out_recv,
     told,
+    far_keyval,
+    far_values_t,
+    far_send,
+    far_recv,
 ):
+    out_p, out_t = out_both.at[0], out_both.at[1]
     ctx = lax.axis_index("ctx")
     uly = lax.axis_index("uly")
     core = lax.rem(uly, 2)
@@ -277,11 +282,11 @@
     def wait_bias(slot):
         pltpu.make_async_copy(bias_rows.at[slot], bias_rows.at[slot], bias_recv.at[slot]).wait()
 
-    def spread_bias(slot):
+    def spread_bias(slot, back, to):
         for t in range(QT):
             for c in range(QT):
-                at = slot * QT + c
-                bias[slot, t, c] = jnp.broadcast_to(bias_rows[slot, t, at : at + 1, :], (8, HEAD))
+                at = back * QT + c
+                bias[to, t, c] = jnp.broadcast_to(bias_rows[slot, t, at : at + 1, :], (8, HEAD))
 
     def forward_own(j):
         wait_query(j, 0)
@@ -300,11 +305,14 @@
             def _():
                 bias_hop(0, 1, 1, ctx, other).start()
 
-            spread_bias(0)
+            spread_bias(0, 0, 0)
 
     def forward_next(j):
         wait_query(j, 2)
-        hop(j, 2, 3, fq_send, behind_or_here, other).start()
+
+        @pl.when((core == 1) | far_by_query(j))
+        def _():
+            hop(j, 2, 3, fq_send, behind_or_here, other).start()
 
         @pl.when(core == 0)
         def _():
@@ -319,7 +327,8 @@
             def _():
                 bias_hop(2, 1, 1, ctx, other).start()
 
-            spread_bias(2)
+            spread_bias(2, 2, 2)
+            spread_bias(2, 3, REACH)
 
     def part_copies(j, src, dst, ctx_to, uly_to):
         return [
@@ -350,7 +359,7 @@
             sink, stats = local.at[j, slot // 2], local_stats.at[j, slot // 2]
         else:
             sink, stats = sent.at[j, slot // 2], sent_stats.at[j, slot // 2]
-        attend(query, keyval, values_t, bias, j, slot, sink, stats)
+        attend(query.at[j, slot], keyval.at[j, 0], values_t.at[j], bias.at[slot], sink, stats)
 
     def absorb(j, which, dst, sink):
         merge(local.at[j, which], local_stats.at[j, which], came.at[j, dst], came_stats.at[j, dst], sink)
@@ -389,17 +398,37 @@
 
     for step in range(1, 4):
         bias_copy(step).start()
+    def far_by_query(j):
+        return look_up(MEET, j) == 0
+
+    def keys_ahead(j):
+        return pltpu.make_async_remote_copy(
+            src_ref=keyval.at[j],
+            dst_ref=far_keyval.at[j],
+            send_sem=far_send.at[j],
+            recv_sem=far_recv.at[j],
+            device_id=(ahead, other),
+            device_id_type=MESH,
+        )
+
     def take_kv(j):
         pltpu.make_async_copy(keyval.at[j], keyval.at[j], kv_recv.at[j]).wait()
         values_t[j] = keyval[j, 1].T
 
-    def work_from(j, slot):
+    def work_far(j):
+        pltpu.make_async_copy(far_keyval.at[j], far_keyval.at[j], far_recv.at[j]).wait()
+        far_values_t[...] = far_keyval[j, 1].T
+        attend(
+            query.at[j, 2], far_keyval.at[j, 0], far_values_t, bias.at[REACH], came.at[j, 1], came_stats.at[j, 1]
+        )
+
+    def work_from(j, slot, first):
         wait_query(j, slot)
 
-        @pl.when(j == 0)
+        @pl.when(j == first)
         def _():
             wait_bias(slot)
-            spread_bias(slot)
+            spread_bias(slot, slot, slot)
 
         work(j, slot)
 
@@ -425,17 +454,26 @@
         j, what = item % 8, item // 8
 
         def attend_pass_previous():
-            work_from(j, 1)
+            work_from(j, 1, jnp.where(core == 0, 0, 0))
             start_part(j, 0, 1 - core, ctx, other)
 
         def attend_pass_far():
-            work_from(j, 3)
-            start_part(j, 1, core, here_or_ahead, other)
+            @pl.when((core == 0) | far_by_query(j))
+            def _():
+                work_from(j, 3, jnp.where(core == 0, 0, 4))
+                start_part(j, 1, core, here_or_ahead, other)
+
+            @pl.when((core == 1) & jnp.logical_not(far_by_query(j)))
+            def _():
+                keys_ahead(j).start()
 
         def pass_on():
+            @pl.when((core == 0) & far_by_query(j))
+            def _():
+                wait_part(j, 1)
+
             @pl.when(core == 0)
             def _():
-                wait_part(j, 1)
                 absorb(j, 1, 1, local.at[j, 1])
 
             wait_part(j, 0)
@@ -465,6 +503,7 @@
             attend_pass_far,
             pass_on,
             finish,
+            lambda: work_far(j),
         )
         for number, step in enumerate(steps):
             pl.when(what == number)(step)
@@ -489,12 +528,21 @@
     def _(j):
         hop(j, 0, 2, zq_send, behind, uly).wait_send()
         hop(j, 0, 1, xq_send, ctx, other).wait_send()
-        hop(j, 2, 3, fq_send, behind_or_here, other).wait_send()
-        for copy in (
-            part_copies(j, 0, 1 - core, ctx, other)
-            + part_copies(j, 1, core, here_or_ahead, other)
-            + part_copies(j, 2, 2, ahead, uly)
-        ):
+
+        @pl.when((core == 1) | far_by_query(j))
+        def _():
+            hop(j, 2, 3, fq_send, behind_or_here, other).wait_send()
+
+        @pl.when((core == 0) | far_by_query(j))
+        def _():
+            for copy in part_copies(j, 1, core, here_or_ahead, other):
+                copy.wait_send()
+
+        @pl.when((core == 1) & jnp.logical_not(far_by_query(j)))
+        def _():
+            keys_ahead(j).wait_send()
+
+        for copy in part_copies(j, 0, 1 - core, ctx, other) + part_copies(j, 2, 2, ahead, uly):
             copy.wait_send()
 
     for t in range(QT):
@@ -513,27 +561,24 @@
     hbm = pl.BlockSpec(memory_space=pltpu.HBM)
     vmem = pl.BlockSpec(memory_space=pltpu.VMEM)
     dma = pltpu.SemaphoreType.DMA
-    return pl.pallas_call(
+    both = pl.pallas_call(
         functools.partial(kernel, n_ctx),
-        out_shape=(
-            jax.ShapeDtypeStruct(query_rows.shape, jnp.bfloat16),
-            jax.ShapeDtypeStruct(query_rows.shape, jnp.bfloat16),
-        ),
+        out_shape=jax.ShapeDtypeStruct((2,) + query_rows.shape, jnp.bfloat16),
         in_specs=[hbm] * 6 + [vmem, vmem, pl.BlockSpec(memory_space=pltpu.SMEM)],
-        out_specs=(anyspace, anyspace),
+        out_specs=anyspace,
         scratch_shapes=[
             pltpu.VMEM((heads, REACH, CT, 2 * HEAD), jnp.bfloat16),
             pltpu.VMEM((heads, 2, CT, 2 * HEAD), jnp.bfloat16),
             pltpu.VMEM((heads, 2 * HEAD, CT), jnp.bfloat16),
             pltpu.VMEM((REACH * QT, HEAD), jnp.float32),
             pltpu.VMEM((REACH, QT, REACH * QT, HEAD), jnp.float32),
-            pltpu.VMEM((REACH, QT, QT, 8, HEAD), jnp.float32),
+            pltpu.VMEM((REACH + 1, QT, QT, 8, HEAD), jnp.float32),
             pltpu.VMEM((heads, 2, 2, HEAD, CT), jnp.float32),
-            pltpu.VMEM((heads, 2, 8, CT), jnp.float32),
+            pltpu.VMEM((heads, 2, 8, PART), jnp.float32),
             pltpu.VMEM((heads, 3, 2, HEAD, CT), jnp.bfloat16),
-            pltpu.VMEM((heads, 3, 8, CT), jnp.float32),
+            pltpu.VMEM((heads, 3, 8, PART), jnp.float32),
             pltpu.VMEM((heads, 3, 2, HEAD, CT), jnp.bfloat16),
-            pltpu.VMEM((heads, 3, 8, CT), jnp.float32),
+            pltpu.VMEM((heads, 3, 8, PART), jnp.float32),
             pltpu.VMEM((heads, 2, CT, HEAD), jnp.bfloat16),
             dma((4, 6)),
             dma((heads, REACH)),
@@ -551,6 +596,10 @@
             dma((QT, 2)),
             dma((2,)),
             pltpu.SemaphoreType.REGULAR,
+            pltpu.VMEM((heads, 2, CT, 2 * HEAD), jnp.bfloat16),
+            pltpu.VMEM((2 * HEAD, CT), jnp.bfloat16),
+            dma((heads,)),
+            dma((heads,)),
         ],
         compiler_params=pltpu.CompilerParams(
             collective_id=0, has_side_effects=True, vmem_limit_bytes=60 * 1024 * 1024
@@ -562,6 +611,7 @@
         ),
         name="band_attention",
     )(query_rows, key_rows, value_rows, query_tan, key_tan, value_tan, tile_query, tile_key, tile_count)
+    return both[0], both[1]
 
 
 def solution(mesh):

time: 90.7 us -> 88.6 us (0.977)
  Pallas kernels: 86.4 us -> 84.8 us
    unnamed x4 -> x0, local copies, waits for them, and re-layouts: 2.87 us -> none
    squeeze x0 -> x1, local copies, waits for them, and re-layouts: none -> 2.42 us  [on_device(): return (both[0], both[1])]
    pallas_call x1, Pallas kernels: 86.4 us -> 84.8 us  [on_device(): pl.pallas_call(functools.partial(kernel, n_ctx), out_shape=jax.ShapeDtype...]
where the time goes in v4:
time: 88.6 us; the launch traced here: 88.5 us
  Pallas kernels  84.8 us (96%)
  local copies, waits for them, and re-layouts  2.42 us (3%)
  between operations  1.29 us (1%)
    pallas_call x1, Pallas kernels, on_device(): pl.pallas_call(functools.partial(kernel, n_ctx), out_shape=jax.ShapeDtype...  84.8 us
    squeeze x1, local copies, waits for them, and re-layouts, on_device(): return (both[0], both[1])  2.42 us

profile of v4, /device:TPU:1, one launch (start us, length us, event | category | flops | bytes accessed | tf_op | source)
XLA Modules:
  0.0 88.5 jit_solution(3208769960693703355)
XLA Ops:
  1.3 84.8 %band_attention.1 = bf16[2,128,2560]{2,1,0:T(8,128)(2,1)} custom-call(bf16[128,2560]{1,0:T(8,128)(2,1)} %q_ref.1, bf16[128,2560]{1,0:T(8,128)(2,1)} %k_ref.1, bf16[128,2560]{1,0:T(8,128)(2,1)} %v_ref.1, bf16[128,2560]{1,0:T(8,128)(2,1)} %qt_ref.1, bf16[128,2560]{1,0:T(8,128)(2,1)} %kt_ref.1, bf16[128,2560]{1,0:T(8,128)(2,1)} %vt_ref.1, s32[1,64]{1,0:T(1,128)} %tq_ref.1, ...), custom_call_target="tpu_custom_call" | custom-call | flops 8053063680 | bytes 3932160 | tf_op jit(solution)/shard_map/band_attention/pallas_call | solution.py:564
  86.1 2.4 %slice_bitcast_fusion = (bf16[128,2560]{1,0:T(8,128)(2,1)}, bf16[128,2560]{1,0:T(8,128)(2,1)}) fusion(bf16[2,128,2560]{2,1,0:T(8,128)(2,1)} %band_attention.1), kind=kLoop, calls=%fused_computation | loop fusion | bytes 2621440 | tf_op jit(solution)/shard_map/squeeze | solution.py:614

commit v5 on v4

--- a/solution.py
+++ b/solution.py
@@ -15,6 +15,7 @@
 CT = 512
 QT = 4
 PART = 256
+HALVES = CT // PART
 MESH = pl.DeviceIdType.MESH
 SCALING = HEAD ** (-0.5)
 LOG2E = math.log2(math.e)
@@ -37,64 +38,61 @@
     return lax.shift_right_logical(word, (at % 4) * 7) % 128
 
 
-def attend(query, keys, values_t, bias, sink, stats):
+def attend(h, query, keys, values_t, bias, sink, stats):
     per = PART // TILE
     nt = (((1,), (1,)), ((), ()))
-    for h in range(CT // PART):
-        cols = pl.ds(h * PART, PART)
-        scores = lax.dot_general(
-            keys[:, :HEAD], query[cols, HEAD:], nt, preferred_element_type=jnp.float32
-        )
-        tans = lax.dot_general(
-            keys[...], query[cols, :], nt, preferred_element_type=jnp.float32
-        )
-        masked = []
-        for c in range(QT):
-            wide = jnp.concatenate([bias[h * per + t, c] for t in range(per)], axis=1)
-            masked.extend([wide] * (TILE // 8))
-        scores = scores * (SCALING * LOG2E) + jnp.concatenate(masked, axis=0)
-        top = jnp.max(scores, axis=0, keepdims=True)
-        weights = jnp.exp2(scores - top)
-        product = weights * tans
-        total = jnp.sum(weights, axis=0, keepdims=True)
-        inverse = 1.0 / total
-        mean_tan = SCALING * jnp.sum(product, axis=0, keepdims=True) * inverse
-        by_weight = jnp.dot(values_t[...], weights.astype(jnp.bfloat16), preferred_element_type=jnp.float32)
-        by_product = jnp.dot(
-            values_t[:HEAD, :], product.astype(jnp.bfloat16), preferred_element_type=jnp.float32
-        )
-        primal = by_weight[:HEAD] * inverse
-        tangent = (SCALING * by_product + by_weight[HEAD:]) * inverse - mean_tan * primal
-        sink[0, :, cols] = primal.astype(sink.dtype)
-        sink[1, :, cols] = tangent.astype(sink.dtype)
-        stats[3 * h : 3 * h + 1, :] = top
-        stats[3 * h + 1 : 3 * h + 2, :] = total
-        stats[3 * h + 2 : 3 * h + 3, :] = mean_tan
-
-
-def merge(own, own_stats, came, came_stats, sink):
-    for h in range(CT // PART):
-        cols = pl.ds(h * PART, PART)
-        top_a, top_b = own_stats[3 * h : 3 * h + 1, :], came_stats[3 * h : 3 * h + 1, :]
-        tan_a, tan_b = own_stats[3 * h + 2 : 3 * h + 3, :], came_stats[3 * h + 2 : 3 * h + 3, :]
-        top = jnp.maximum(top_a, top_b)
-        part_a = own_stats[3 * h + 1 : 3 * h + 2, :] * jnp.exp2(top_a - top)
-        part_b = came_stats[3 * h + 1 : 3 * h + 2, :] * jnp.exp2(top_b - top)
-        total = part_a + part_b
-        inverse = 1.0 / total
-        part_a, part_b = part_a * inverse, part_b * inverse
-        mean_tan = part_a * tan_a + part_b * tan_b
-        primal_a, primal_b = own[0, :, cols], came[0, :, cols].astype(jnp.float32)
-        tangent_a, tangent_b = own[1, :, cols], came[1, :, cols].astype(jnp.float32)
-        primal = part_a * primal_a + part_b * primal_b
-        tangent = part_a * (tangent_a + (tan_a - mean_tan) * primal_a) + part_b * (
-            tangent_b + (tan_b - mean_tan) * primal_b
-        )
-        sink[0, :, cols] = primal.astype(sink.dtype)
-        sink[1, :, cols] = tangent.astype(sink.dtype)
-        own_stats[3 * h : 3 * h + 1, :] = top
-        own_stats[3 * h + 1 : 3 * h + 2, :] = total
-        own_stats[3 * h + 2 : 3 * h + 3, :] = mean_tan
+    cols = pl.ds(h * PART, PART)
+    scores = lax.dot_general(
+        keys[:, :HEAD], query[cols, HEAD:], nt, preferred_element_type=jnp.float32
+    )
+    tans = lax.dot_general(
+        keys[...], query[cols, :], nt, preferred_element_type=jnp.float32
+    )
+    masked = []
+    for c in range(QT):
+        wide = jnp.concatenate([bias[h * per + t, c] for t in range(per)], axis=1)
+        masked.extend([wide] * (TILE // 8))
+    scores = scores * (SCALING * LOG2E) + jnp.concatenate(masked, axis=0)
+    top = jnp.max(scores, axis=0, keepdims=True)
+    weights = jnp.exp2(scores - top)
+    product = weights * tans
+    total = jnp.sum(weights, axis=0, keepdims=True)
+    inverse = 1.0 / total
+    mean_tan = SCALING * jnp.sum(product, axis=0, keepdims=True) * inverse
+    by_weight = jnp.dot(values_t[...], weights.astype(jnp.bfloat16), preferred_element_type=jnp.float32)
+    by_product = jnp.dot(
+        values_t[:HEAD, :], product.astype(jnp.bfloat16), preferred_element_type=jnp.float32
+    )
+    primal = by_weight[:HEAD] * inverse
+    tangent = (SCALING * by_product + by_weight[HEAD:]) * inverse - mean_tan * primal
+    sink[h, 0] = primal.astype(sink.dtype)
+    sink[h, 1] = tangent.astype(sink.dtype)
+    stats[h, 0:1, :] = top
+    stats[h, 1:2, :] = total
+    stats[h, 2:3, :] = mean_tan
+
+
+def merge(h, own, own_stats, came, came_stats, sink):
+    top_a, top_b = own_stats[h, 0:1, :], came_stats[h, 0:1, :]
+    tan_a, tan_b = own_stats[h, 2:3, :], came_stats[h, 2:3, :]
+    top = jnp.maximum(top_a, top_b)
+    part_a = own_stats[h, 1:2, :] * jnp.exp2(top_a - top)
+    part_b = came_stats[h, 1:2, :] * jnp.exp2(top_b - top)
+    total = part_a + part_b
+    inverse = 1.0 / total
+    part_a, part_b = part_a * inverse, part_b * inverse
+    mean_tan = part_a * tan_a + part_b * tan_b
+    primal_a, primal_b = own[h, 0], came[h, 0].astype(jnp.float32)
+    tangent_a, tangent_b = own[h, 1], came[h, 1].astype(jnp.float32)
+    primal = part_a * primal_a + part_b * primal_b
+    tangent = part_a * (tangent_a + (tan_a - mean_tan) * primal_a) + part_b * (
+        tangent_b + (tan_b - mean_tan) * primal_b
+    )
+    sink[h, 0] = primal.astype(sink.dtype)
+    sink[h, 1] = tangent.astype(sink.dtype)
+    own_stats[h, 0:1, :] = top
+    own_stats[h, 1:2, :] = total
+    own_stats[h, 2:3, :] = mean_tan
 
 
 def kernel(
@@ -330,13 +328,13 @@
             spread_bias(2, 2, 2)
             spread_bias(2, 3, REACH)
 
-    def part_copies(j, src, dst, ctx_to, uly_to):
+    def part_copies(h, j, src, dst, ctx_to, uly_to):
         return [
             pltpu.make_async_remote_copy(
-                src_ref=a.at[j, src],
-                dst_ref=b.at[j, dst],
-                send_sem=ss.at[j, src],
-                recv_sem=rs.at[j, dst],
+                src_ref=a.at[j, src, h],
+                dst_ref=b.at[j, dst, h],
+                send_sem=ss.at[j, src, h],
+                recv_sem=rs.at[j, dst, h],
                 device_id=(ctx_to, uly_to),
                 device_id_type=MESH,
             )
@@ -350,23 +348,33 @@
         for copy in part_copies(*args):
             copy.start()
 
-    def wait_part(j, dst):
-        pltpu.make_async_copy(came.at[j, dst], came.at[j, dst], part_recv.at[j, dst]).wait()
-        pltpu.make_async_copy(came_stats.at[j, dst], came_stats.at[j, dst], stat_recv.at[j, dst]).wait()
-
-    def work(j, slot):
-        if slot % 2 == 0:
-            sink, stats = local.at[j, slot // 2], local_stats.at[j, slot // 2]
-        else:
-            sink, stats = sent.at[j, slot // 2], sent_stats.at[j, slot // 2]
-        attend(query.at[j, slot], keyval.at[j, 0], values_t.at[j], bias.at[slot], sink, stats)
-
-    def absorb(j, which, dst, sink):
-        merge(local.at[j, which], local_stats.at[j, which], came.at[j, dst], came_stats.at[j, dst], sink)
-
-    def send_out(j):
+    def wait_part(h, j, dst):
+        for ref, sem in ((came, part_recv), (came_stats, stat_recv)):
+            pltpu.make_async_copy(ref.at[j, dst, h], ref.at[j, dst, h], sem.at[j, dst, h]).wait()
+
+    def work(j, slot, *way):
+        kept = slot % 2 == 0
+        place = (j, slot // 2)
+        sink, stats = (local, local_stats) if kept else (sent, sent_stats)
+        for h in range(HALVES):
+            attend(
+                h,
+                query.at[j, slot],
+                keyval.at[j, 0],
+                values_t.at[j],
+                bias.at[slot],
+                sink.at[place],
+                stats.at[place],
+            )
+            if not kept:
+                start_part(h, j, slot // 2, *way)
+
+    def absorb(h, j, which, dst, sink):
+        merge(h, local.at[j, which], local_stats.at[j, which], came.at[j, dst], came_stats.at[j, dst], sink)
+
+    def send_out(h, j):
         cols = pl.ds(pl.multiple_of((y * LOCAL_HEADS + j) * HEAD, HEAD), HEAD)
-        for t in range(QT):
+        for t in range(h * PART // TILE, (h + 1) * PART // TILE):
             def remote():
                 for a, out in enumerate((out_p, out_t)):
                     pltpu.make_async_remote_copy(
@@ -418,11 +426,18 @@
     def work_far(j):
         pltpu.make_async_copy(far_keyval.at[j], far_keyval.at[j], far_recv.at[j]).wait()
         far_values_t[...] = far_keyval[j, 1].T
-        attend(
-            query.at[j, 2], far_keyval.at[j, 0], far_values_t, bias.at[REACH], came.at[j, 1], came_stats.at[j, 1]
-        )
-
-    def work_from(j, slot, first):
+        for h in range(HALVES):
+            attend(
+                h,
+                query.at[j, 2],
+                far_keyval.at[j, 0],
+                far_values_t,
+                bias.at[REACH],
+                came.at[j, 1],
+                came_stats.at[j, 1],
+            )
+
+    def work_from(j, slot, first, *way):
         wait_query(j, slot)
 
         @pl.when(j == first)
@@ -430,7 +445,7 @@
             wait_bias(slot)
             spread_bias(slot, slot, slot)
 
-        work(j, slot)
+        work(j, slot, *way)
 
     @pl.loop(0, 2 * LOCAL_HEADS)
     def _(at):
@@ -454,44 +469,45 @@
         j, what = item % 8, item // 8
 
         def attend_pass_previous():
-            work_from(j, 1, jnp.where(core == 0, 0, 0))
-            start_part(j, 0, 1 - core, ctx, other)
+            work_from(j, 1, jnp.where(core == 0, 0, 0), 1 - core, ctx, other)
 
         def attend_pass_far():
             @pl.when((core == 0) | far_by_query(j))
             def _():
-                work_from(j, 3, jnp.where(core == 0, 0, 4))
-                start_part(j, 1, core, here_or_ahead, other)
+                work_from(j, 3, jnp.where(core == 0, 0, 4), core, here_or_ahead, other)
 
             @pl.when((core == 1) & jnp.logical_not(far_by_query(j)))
             def _():
                 keys_ahead(j).start()
 
         def pass_on():
-            @pl.when((core == 0) & far_by_query(j))
-            def _():
-                wait_part(j, 1)
-
-            @pl.when(core == 0)
-            def _():
-                absorb(j, 1, 1, local.at[j, 1])
-
-            wait_part(j, 0)
-            absorb(j, 1, 0, sent.at[j, 2])
-            sent_stats[j, 2] = local_stats[j, 1]
-            start_part(j, 2, 2, ahead, uly)
+            for h in range(HALVES):
+                @pl.when((core == 0) & far_by_query(j))
+                def _():
+                    wait_part(h, j, 1)
+
+                @pl.when(core == 0)
+                def _():
+                    absorb(h, j, 1, 1, local.at[j, 1])
+
+                wait_part(h, j, 0)
+                absorb(h, j, 1, 0, sent.at[j, 2])
+                sent_stats[j, 2, h] = local_stats[j, 1, h]
+                start_part(h, j, 2, 2, ahead, uly)
 
         def finish():
-            @pl.when(core == 1)
-            def _():
-                wait_part(j, 1)
-                absorb(j, 0, 1, local.at[j, 0])
-
-            wait_part(j, 2)
-            absorb(j, 0, 2, local.at[j, 0])
-            outbuf[j, 0] = local[j, 0, 0].T.astype(jnp.bfloat16)
-            outbuf[j, 1] = local[j, 0, 1].T.astype(jnp.bfloat16)
-            send_out(j)
+            for h in range(HALVES):
+                @pl.when(core == 1)
+                def _():
+                    wait_part(h, j, 1)
+                    absorb(h, j, 0, 1, local.at[j, 0])
+
+                wait_part(h, j, 2)
+                absorb(h, j, 0, 2, local.at[j, 0])
+                rows = pl.ds(h * PART, PART)
+                outbuf[j, 0, rows, :] = local[j, 0, h, 0].T.astype(jnp.bfloat16)
+                outbuf[j, 1, rows, :] = local[j, 0, h, 1].T.astype(jnp.bfloat16)
+                send_out(h, j)
 
         steps = (
             lambda: forward_own(j),
@@ -535,15 +551,17 @@
 
         @pl.when((core == 0) | far_by_query(j))
         def _():
-            for copy in part_copies(j, 1, core, here_or_ahead, other):
+            for h in range(HALVES):
+                for copy in part_copies(h, j, 1, core, here_or_ahead, other):
+                    copy.wait_send()
+
+        @pl.when((core == 1) & jnp.logical_not(far_by_query(j)))
+        def _():
+            keys_ahead(j).wait_send()
+
+        for h in range(HALVES):
+            for copy in part_copies(h, j, 0, 1 - core, ctx, other) + part_copies(h, j, 2, 2, ahead, uly):
                 copy.wait_send()
-
-        @pl.when((core == 1) & jnp.logical_not(far_by_query(j)))
-        def _():
-            keys_ahead(j).wait_send()
-
-        for copy in part_copies(j, 0, 1 - core, ctx, other) + part_copies(j, 2, 2, ahead, uly):
-            copy.wait_send()
 
     for t in range(QT):
         @pl.when(jnp.logical_not(at_home & (uly == t)))
@@ -573,12 +591,12 @@
             pltpu.VMEM((REACH * QT, HEAD), jnp.float32),
             pltpu.VMEM((REACH, QT, REACH * QT, HEAD), jnp.float32),
             pltpu.VMEM((REACH + 1, QT, QT, 8, HEAD), jnp.float32),
-            pltpu.VMEM((heads, 2, 2, HEAD, CT), jnp.float32),
-            pltpu.VMEM((heads, 2, 8, PART), jnp.float32),
-            pltpu.VMEM((heads, 3, 2, HEAD, CT), jnp.bfloat16),
-            pltpu.VMEM((heads, 3, 8, PART), jnp.float32),
-            pltpu.VMEM((heads, 3, 2, HEAD, CT), jnp.bfloat16),
-            pltpu.VMEM((heads, 3, 8, PART), jnp.float32),
+            pltpu.VMEM((heads, 2, HALVES, 2, HEAD, PART), jnp.float32),
+            pltpu.VMEM((heads, 2, HALVES, 8, PART), jnp.float32),
+            pltpu.VMEM((heads, 3, HALVES, 2, HEAD, PART), jnp.bfloat16),
+            pltpu.VMEM((heads, 3, HALVES, 8, PART), jnp.float32),
+            pltpu.VMEM((heads, 3, HALVES, 2, HEAD, PART), jnp.bfloat16),
+            pltpu.VMEM((heads, 3, HALVES, 8, PART), jnp.float32),
             pltpu.VMEM((heads, 2, CT, HEAD), jnp.bfloat16),
             dma((4, 6)),
             dma((heads, REACH)),
@@ -589,10 +607,10 @@
             dma((4,)),
             dma((3,)),
             dma((REACH,)),
-            dma((heads, 3)),
-            dma((heads, 3)),
-            dma((heads, 3)),
-            dma((heads, 3)),
+            dma((heads, 3, HALVES)),
+            dma((heads, 3, HALVES)),
+            dma((heads, 3, HALVES)),
+            dma((heads, 3, HALVES)),
             dma((QT, 2)),
             dma((2,)),
             pltpu.SemaphoreType.REGULAR,

time: 88.6 us -> 86.6 us (0.977)
  Pallas kernels: 84.8 us -> 82.8 us
    pallas_call x1, Pallas kernels: 84.8 us -> 82.8 us  [on_device(): pl.pallas_call(functools.partial(kernel, n_ctx), out_shape=jax.ShapeDtype...]
where the time goes in v5:
time: 86.6 us; the launch traced here: 86.5 us
  Pallas kernels  82.8 us (96%)
  local copies, waits for them, and re-layouts  2.42 us (3%)
  between operations  1.29 us (1%)
    pallas_call x1, Pallas kernels, on_device(): pl.pallas_call(functools.partial(kernel, n_ctx), out_shape=jax.ShapeDtype...  82.8 us
    squeeze x1, local copies, waits for them, and re-layouts, on_device(): return (both[0], both[1])  2.42 us

profile of v5, /device:TPU:1, one launch (start us, length us, event | category | flops | bytes accessed | tf_op | source)
XLA Modules:
  0.0 86.5 jit_solution(11885017951809340983)
XLA Ops:
  1.3 82.8 %band_attention.1 = bf16[2,128,2560]{2,1,0:T(8,128)(2,1)} custom-call(bf16[128,2560]{1,0:T(8,128)(2,1)} %q_ref.1, bf16[128,2560]{1,0:T(8,128)(2,1)} %k_ref.1, bf16[128,2560]{1,0:T(8,128)(2,1)} %v_ref.1, bf16[128,2560]{1,0:T(8,128)(2,1)} %qt_ref.1, bf16[128,2560]{1,0:T(8,128)(2,1)} %kt_ref.1, bf16[128,2560]{1,0:T(8,128)(2,1)} %vt_ref.1, s32[1,64]{1,0:T(1,128)} %tq_ref.1, ...), custom_call_target="tpu_custom_call" | custom-call | flops 8053063680 | bytes 3932160 | tf_op jit(solution)/shard_map/band_attention/pallas_call | solution.py:582
  84.0 2.4 %slice_bitcast_fusion = (bf16[128,2560]{1,0:T(8,128)(2,1)}, bf16[128,2560]{1,0:T(8,128)(2,1)}) fusion(bf16[2,128,2560]{2,1,0:T(8,128)(2,1)} %band_attention.1), kind=kLoop, calls=%fused_computation | loop fusion | bytes 2621440 | tf_op jit(solution)/shard_map/squeeze | solution.py:632

commit v6 on v5

--- a/solution.py
+++ b/solution.py
@@ -22,11 +22,11 @@
 NEG = -1e30
 
 
-MEET = [1, 0, 1, 0, 0]
-SEND_EVEN = [4, 0, 8, 2, 3, 10, 12, 1, 11, 9]
-SEND_ODD = [8, 0, 10, 12, 4, 2, 3, 11, 1, 9]
-PLAN_EVEN = [0, 16, 4, 8, 24, 2, 40, 48, 12, 3, 32, 10, 18, 72, 42, 56, 74, 58, 20, 44, 26, 11, 60, 1, 52, 36, 50, 34, 28, 64, 9, 19, 51, 66, 35, 68, 43, 59, 27, 17, 33, 49, 41, 67, 57, 25, 65]
-PLAN_ODD = [16, 48, 0, 18, 50, 8, 40, 32, 56, 20, 24, 52, 4, 2, 34, 26, 12, 3, 36, 44, 10, 42, 60, 11, 19, 43, 58, 64, 51, 28, 1, 27, 59, 35, 68, 66, 17, 49, 9, 25, 41, 67, 57, 33, 65, 80, 80]
+MEET = [1, 0, 0, 1, 0]
+SEND_EVEN = [0, 4, 8, 2, 12, 1, 3, 9, 10, 11]
+SEND_ODD = [8, 0, 11, 4, 12, 10, 1, 9, 3, 2]
+PLAN_EVEN = [0, 4, 16, 8, 12, 2, 32, 40, 48, 72, 56, 1, 20, 10, 24, 52, 9, 28, 36, 44, 17, 33, 25, 60, 18, 3, 42, 58, 26, 64, 49, 68, 19, 27, 41, 57, 51, 11, 66, 50, 75, 35, 43, 65, 59, 34, 67]
+PLAN_ODD = [16, 48, 0, 19, 51, 8, 40, 32, 4, 56, 24, 12, 20, 52, 44, 36, 60, 18, 1, 50, 28, 34, 9, 17, 49, 3, 41, 33, 2, 68, 57, 11, 64, 43, 10, 42, 59, 25, 65, 26, 58, 35, 27, 67, 66, 80, 80]
 
 
 def look_up(table, at):
@@ -496,12 +496,13 @@
                 start_part(h, j, 2, 2, ahead, uly)
 
         def finish():
-            for h in range(HALVES):
-                @pl.when(core == 1)
-                def _():
+            @pl.when(core == 1)
+            def _():
+                for h in range(HALVES):
                     wait_part(h, j, 1)
                     absorb(h, j, 0, 1, local.at[j, 0])
 
+            for h in range(HALVES):
                 wait_part(h, j, 2)
                 absorb(h, j, 0, 2, local.at[j, 0])
                 rows = pl.ds(h * PART, PART)

time: 86.6 us -> 86.3 us (level)
  no operation moved by 1% of the time
where the time goes in v6:
time: 86.3 us; the launch traced here: 86.2 us
  Pallas kernels  82.4 us (95%)
  local copies, waits for them, and re-layouts  2.42 us (3%)
  between operations  1.29 us (1%)
    pallas_call x1, Pallas kernels, on_device(): pl.pallas_call(functools.partial(kernel, n_ctx), out_shape=jax.ShapeDtype...  82.4 us
    squeeze x1, local copies, waits for them, and re-layouts, on_device(): return (both[0], both[1])  2.42 us

profile of v6, /device:TPU:1, one launch (start us, length us, event | category | flops | bytes accessed | tf_op | source)
XLA Modules:
  0.0 86.2 jit_solution(12784869035606489617)
XLA Ops:
  1.3 82.4 %band_attention.1 = bf16[2,128,2560]{2,1,0:T(8,128)(2,1)} custom-call(bf16[128,2560]{1,0:T(8,128)(2,1)} %q_ref.1, bf16[128,2560]{1,0:T(8,128)(2,1)} %k_ref.1, bf16[128,2560]{1,0:T(8,128)(2,1)} %v_ref.1, bf16[128,2560]{1,0:T(8,128)(2,1)} %qt_ref.1, bf16[128,2560]{1,0:T(8,128)(2,1)} %kt_ref.1, bf16[128,2560]{1,0:T(8,128)(2,1)} %vt_ref.1, s32[1,64]{1,0:T(1,128)} %tq_ref.1, ...), custom_call_target="tpu_custom_call" | custom-call | flops 8053063680 | bytes 3932160 | tf_op jit(solution)/shard_map/band_attention/pallas_call | solution.py:583
  83.7 2.4 %slice_bitcast_fusion = (bf16[128,2560]{1,0:T(8,128)(2,1)}, bf16[128,2560]{1,0:T(8,128)(2,1)}) fusion(bf16[2,128,2560]{2,1,0:T(8,128)(2,1)} %band_attention.1), kind=kLoop, calls=%fused_computation | loop fusion | bytes 2621440 | tf_op jit(solution)/shard_map/squeeze | solution.py:633
